TPU v7x, 32 devices: a whole 2x2x4 slice. The times are simulated.
32 devices in a mesh: blk: 4 (over y, x), grp: 8 (over z, core).
Axes of the slice: x: 2, y: 2, z: 4, core: 2. Of those that a mesh axis runs over, the one named last changes fastest.
Arguments:
- record: bfloat16 [16448, 8192], P(None, ('blk', 'grp')), may hold values from -400 to 400
- owner_order: int32 [4, 4], replicated, may hold values from 0 to 7, as said below
Outputs:
- cross_spectra: bfloat16 [4, 2, 16, 8192, 256], P(None, None, None, ('blk', 'grp'))
Inputs may be any that keep to these rules, and one draw needn't show every extreme that they name: `owner_order`: a channel block position within a group.
All inputs are finite; a program needn't handle non-finite values.
Results may differ from a plain program's by a relative error of at most 0.0071.
Values may be sent and summed in bfloat16 or wider, within the bound.
No kernel may reach another device: no remote copies, remote signals or barrier semaphores. Data moves between devices by JAX's collectives and lax.ppermute only.
A program may use at most 192 MiB of HBM per device.

v0:
```python
import math

import jax
import jax.numpy as jnp
from jax import lax
from jax.sharding import PartitionSpec as P

WIN = 256
NS = 128
NB = 16
BIN_LO = 8
ROUNDS = 4
HOP = 64


def shifted(value, axis, steps):
    count = lax.axis_size(axis)
    pairs = [(source, (source + steps) % count) for source in range(count)]
    return lax.ppermute(value, axis, pairs)


def broadcast(value, axis, source):
    kept = jnp.where(lax.axis_index(axis) == source, value, 0).astype(value.dtype)
    return lax.psum(kept, axis)


def band_table():
    sample_index = jnp.arange(NS, dtype=jnp.int32)
    bin_index = BIN_LO + jnp.arange(NB, dtype=jnp.int32)
    phase_int = bin_index[:, None] * sample_index[None, :] % NS
    phase = phase_int.astype(jnp.float32) * (2.0 * math.pi / NS)
    taper = 0.5 - 0.5 * jnp.cos(sample_index.astype(jnp.float32) * (2.0 * math.pi / NS))
    scale = 1.0 / math.sqrt(3.0 * NS / 8.0)
    real_rows = taper[None, :] * jnp.cos(phase) * scale
    imag_rows = -taper[None, :] * jnp.sin(phase) * scale
    return jnp.concatenate([real_rows, imag_rows], axis=0).astype(jnp.bfloat16)


def block_spectra(record):
    table = band_table()
    halves = record.reshape(WIN + 1, HOP, record.shape[1])
    first_half = jnp.einsum(
        "kn,hnc->hkc", table[:, :HOP], halves, preferred_element_type=jnp.float32
    )
    second_half = jnp.einsum(
        "kn,hnc->hkc", table[:, HOP:], halves, preferred_element_type=jnp.float32
    )
    wide_halves = halves.astype(jnp.float32)
    half_energy = jnp.sum(wide_halves * wide_halves, axis=1)
    window_rms = jnp.sqrt((half_energy[:-1] + half_energy[1:]) / NS + 1e-05)
    raw = first_half[:-1] + second_half[1:]
    return (raw / window_rms[:, None, :]).astype(jnp.bfloat16)


def cross_stack(own, other):
    real_own, imag_own = (own[:, :NB], own[:, NB:])
    real_other, imag_other = (other[:, :NB], other[:, NB:])
    real_part = jnp.einsum("wfi,wfj->fij", real_own, real_other, preferred_element_type=jnp.float32)
    real_part = real_part + jnp.einsum(
        "wfi,wfj->fij", imag_own, imag_other, preferred_element_type=jnp.float32
    )
    imag_part = jnp.einsum("wfi,wfj->fij", imag_own, real_other, preferred_element_type=jnp.float32)
    imag_part = imag_part - jnp.einsum(
        "wfi,wfj->fij", real_own, imag_other, preferred_element_type=jnp.float32
    )
    return jnp.stack([real_part, imag_part], axis=0) / math.sqrt(WIN)


def body(record, owner_order):
    spectra = block_spectra(record)
    my_group = lax.axis_index("blk")
    results = []
    resident = spectra
    for round_index in range(ROUNDS):
        if round_index > 0:
            resident = shifted(resident, "blk", 1)
        owner_rank = owner_order[round_index, my_group]
        received = broadcast(resident, "grp", owner_rank)
        results.append(cross_stack(spectra, received))
    return jnp.stack(results, axis=0).astype(jnp.bfloat16)


def solution(mesh):
    placed = (P(None, ("blk", "grp")), P())
    return jax.shard_map(
        body,
        mesh=mesh,
        in_specs=placed,
        out_specs=P(None, None, None, ("blk", "grp"), None),
        check_vma=False,
    )
```

profile of v0, /device:TPU:0, one launch (start us, length us, event | category | flops | bytes accessed | tf_op | source)
XLA Modules:
  0.0 718.4 jit_solution(2890194203787881614)
XLA Ops:
  6.6 6.8 multiply_reduce_fusion
  13.6 4.8 convolution_bitcast_fusion
  18.3 4.6 convolution_bitcast_fusion.1
  23.0 0.7 constant_dynamic-slice_fusion.2
  24.3 8.7 %broadcast_select_fusion.3 = (bf16[256,32,256]{2,1,0:T(8,128)(2,1)}, bf16[256,32,256]{2,1,0:T(8,128)(2,1)S(1)}) fusion(pred[]{:T(512)S(6)} %eq.14, f32[256,256]{1,0:T(8,128)S(1)} %fusion.32, f32[257,32,256]{2,1,0:T(8,128)} %convolution_bitcast_fusion, f32[257,32,256]{2,1,0:T(8,128)} %convolution_bitcast_fusion.1), kind=kLoop, calls=%fused_computation.24 | loop fusion | flops 8388608 | bytes 25427968 | tf_op jit(solution)/shard_map/jit(_where)/select_n | solution.py:23
  33.0 2.0 copy-done.4
  35.0 2.9 collective-permute-start
  37.9 91.5 %collective-permute-done = bf16[256,32,256]{2,1,0:T(8,128)(2,1)S(1)} collective-permute-done((bf16[256,32,256]{2,1,0:T(8,128)(2,1)S(1)}, bf16[256,32,256]{2,1,0:T(8,128)(2,1)S(1)}, u32[]{:S(2)}, u32[]{:S(2)}) %collective-permute-start) | collective-permute-done | bytes 4194336 | tf_op jit(solution)/shard_map/ppermute | solution.py:19
  129.5 2.0 copy-done.8
  131.4 0.8 collective-permute-start.1
  132.2 92.0 %collective-permute-done.1 = bf16[256,32,256]{2,1,0:T(8,128)(2,1)} collective-permute-done((bf16[256,32,256]{2,1,0:T(8,128)(2,1)S(1)}, bf16[256,32,256]{2,1,0:T(8,128)(2,1)}, u32[]{:S(2)}, u32[]{:S(2)}) %collective-permute-start.1) | collective-permute-done | bytes 4194336 | tf_op jit(solution)/shard_map/ppermute | solution.py:19
  226.1 2.3 broadcast_select_fusion.2
  228.4 2.2 broadcast_select_fusion.1
  230.7 85.6 %collective-permute-done.2 = bf16[256,32,256]{2,1,0:T(8,128)(2,1)} collective-permute-done((bf16[256,32,256]{2,1,0:T(8,128)(2,1)}, bf16[256,32,256]{2,1,0:T(8,128)(2,1)}, u32[]{:S(2)}, u32[]{:S(2)}) %collective-permute-start.2) | collective-permute-done | bytes 4194336 | tf_op jit(solution)/shard_map/ppermute | solution.py:19
  316.3 4.4 broadcast_select_fusion
  320.7 4.6 fusion.54
  325.3 3.0 copy.5
  328.3 4.3 copy.3
  332.6 321.0 %all-reduce.3.cloned.1.call-done = (bf16[256,32,256]{2,1,0:T(8,128)(2,1)}, bf16[256,32,256]{2,1,0:T(8,128)(2,1)}, bf16[256,32,256]{2,1,0:T(8,128)(2,1)}, bf16[256,32,256]{2,1,0:T(8,128)(2,1)}) async-done(((bf16[256,32,256]{2,1,0:T(8,128)(2,1)}, bf16[256,32,256]{2,1,0:T(8,128)(2,1)}, bf16[256,32,256]{2,1,0:T(8,128)(2,1)}, bf16[256,32,256]{2,1,0:T(8,128)(2,1)}), (bf16[256,32,256]{2,1,0:T(8,128)(2,1)}, ...) | async-done | bytes 16777232 | tf_op jit(solution)/shard_map/psum | solution.py:24
  653.5 2.7 fusion.53
  656.4 1.0 fusion.6
  657.4 1.0 fusion.8
  658.4 1.2 copy-done.7
  659.6 0.3 fusion.52
  659.9 3.0 fusion.12
  662.9 1.0 fusion.14
  663.9 1.2 copy-done.6
  665.4 3.0 fusion.18
  668.4 1.0 fusion.20
  669.4 2.5 fusion.50
  671.9 2.9 fusion.26
  674.9 2.9 fusion.28
  677.8 1.1 subtract_bitcast_fusion
  678.9 1.0 add_bitcast_fusion
  679.9 1.1 copy-done.3
  681.1 1.2 subtract_bitcast_fusion.1
  682.2 1.3 add_bitcast_fusion.1
  683.5 3.4 subtract_bitcast_fusion.2
  686.8 1.0 add_bitcast_fusion.2
  687.9 3.4 subtract_bitcast_fusion.3
  691.3 5.3 add_bitcast_fusion.3
  696.6 2.5 fusion.5
  699.1 1.0 fusion.4
  700.2 1.1 fusion.3
  701.3 1.1 copy-done.2
  702.4 1.0 fusion.2
  703.4 1.1 copy-done.5
  704.5 7.0 pad_maximum_fusion
  (21 shorter events, 0.8 us)
Async XLA Ops:
  6.5 647.0 %all-reduce.3.cloned.1.call-start = ((), (), s32[]{:S(2)}) async-start(), calls=%async_computation | async-start | bytes 33554432 | tf_op jit(solution)/shard_map/psum | solution.py:24
  6.6 7.0 copy-start.1
  18.3 4.7 copy-start.9
  33.0 2.0 copy-start.4
  35.0 94.5 %collective-permute-start = (bf16[256,32,256]{2,1,0:T(8,128)(2,1)S(1)}, bf16[256,32,256]{2,1,0:T(8,128)(2,1)S(1)}, u32[]{:S(2)}, u32[]{:S(2)}) collective-permute-start(bf16[256,32,256]{2,1,0:T(8,128)(2,1)S(1)} %get-tuple-element.10), channel_id=1, source_target_pairs={{0,8},{8,16},{16,24},{24,0},{1,9},{9,17},{17,25},{25,1},{2,10},{10... | collective-permute-start | bytes 12582920 | tf_op jit(solution)/shard_map/ppermute | solution.py:19
  129.5 2.0 copy-start.8
  131.4 92.8 %collective-permute-start.1 = (bf16[256,32,256]{2,1,0:T(8,128)(2,1)S(1)}, bf16[256,32,256]{2,1,0:T(8,128)(2,1)}, u32[]{:S(2)}, u32[]{:S(2)}) collective-permute-start(bf16[256,32,256]{2,1,0:T(8,128)(2,1)S(1)} %collective-permute-done), channel_id=1, source_target_pairs={{0,8},{8,16},{16,24},{24,0},{1,9},{9,17},{17,25},{25,1},{2,10},{10... | collective-permute-start | bytes 12582920 | tf_op jit(solution)/shard_map/ppermute | solution.py:19
  224.2 92.1 %collective-permute-start.2 = (bf16[256,32,256]{2,1,0:T(8,128)(2,1)}, bf16[256,32,256]{2,1,0:T(8,128)(2,1)}, u32[]{:S(2)}, u32[]{:S(2)}) collective-permute-start(bf16[256,32,256]{2,1,0:T(8,128)(2,1)} %collective-permute-done.1), channel_id=1, source_target_pairs={{0,8},{8,16},{16,24},{24,0},{1,9},{9,17},{17,25},{25,1},{2,10},{10... | collective-permute-start | bytes 12582920 | tf_op jit(solution)/shard_map/ppermute | solution.py:19
  653.5 2.9 copy-start
  657.4 2.2 copy-start.7
  662.9 2.2 copy-start.6
  678.9 2.2 copy-start.3
  700.2 2.2 copy-start.2
  702.4 2.2 copy-start.5
Sparse Core Ops, SparseCore 0:
  320.8 332.6 all-reduce.2
where the time goes:
time: 719 us; the launch traced here: 718 us
  waiting for transfers between devices  590 us (82%)
  matrix products  42.6 us (6%)
  other arithmetic  37.4 us (5%)
  local copies, waits for them, and re-layouts  28.4 us (4%)
  between operations  16.1 us (2%)
    psum x1, waiting for transfers between devices, broadcast(): return lax.psum(kept, axis)  321 us
    ppermute x3, waiting for transfers between devices, shifted(): return lax.ppermute(value, axis, pairs)  269 us
    select_n x4, other arithmetic, broadcast(): jnp.where(lax.axis_index(axis) == source, value, 0).astype(value.dtype)  17.6 us
  transfers between devices with their start and end apart: 4, of which 4 were waited for; matrix products, arithmetic and copies ran while one was open for 2% of the time, Pallas kernels for 0%

commit v1 on v0

v1 whole, which is shorter than its diff:
```python
import functools
import math

import jax
import jax.numpy as jnp
import numpy as np
from jax import lax
from jax.experimental import pallas as pl
from jax.experimental.pallas import tpu as pltpu
from jax.sharding import PartitionSpec as P

WIN = 256
NS = 128
NB = 16
BIN_LO = 8
ROUNDS = 4
HOP = 64
WG = 16
CORES = 2
HALF = NB // CORES
FIRST = 2
LAG = 2
ORDER = (1, 3, 2, 0)
HBM = pltpu.MemorySpace.HBM


def band_table():
    n = np.arange(NS)
    q = BIN_LO + np.arange(NB)
    phase = ((q[:, None] * n[None, :]) % NS) * (2.0 * math.pi / NS)
    taper = 0.5 - 0.5 * np.cos(n * (2.0 * math.pi / NS))
    scale = 1.0 / math.sqrt(3.0 * NS / 8.0)
    real = taper * np.cos(phase) * scale
    imag = -taper * np.sin(phase) * scale
    return np.stack([real, imag], axis=1).astype(np.float32)


def banded(bins):
    table = band_table()[bins]
    out = np.zeros((len(bins), 2, WG, (WG + 1) * HOP), np.float32)
    for w in range(WG):
        out[:, :, w, w * HOP : w * HOP + NS] = table
    return out.reshape(len(bins) * 2 * WG, (WG + 1) * HOP)


def tables(lo, hi):
    both = [banded(np.arange(h * HALF + lo, h * HALF + hi)) for h in range(CORES)]
    return jnp.asarray(np.stack(both).astype(jnp.bfloat16))


def half_energy(x):
    wide = x.astype(jnp.float32)
    return jnp.sum((wide * wide).reshape(-1, HOP, x.shape[-1]), axis=1)


def band_kernel(first, core_ref, main_ref, halo_ref, mine_table, other_table, *refs):
    main, halo = main_ref[...], halo_ref[...]
    if first:
        mine_ref, other_ref, inv_ref = refs
        energy = half_energy(main)
        later = jnp.concatenate([energy[1:], half_energy(halo)], axis=0)
        inv = 1.0 / jnp.sqrt((energy + later) / NS + 1e-05)
        inv_ref[...] = inv
    else:
        inv_ref, mine_ref, other_ref = refs
        inv = inv_ref[...]
    split = WG * HOP
    for table, out in ((mine_table, mine_ref), (other_table, other_ref)):
        raw = jnp.dot(table[0, :, :split], main, preferred_element_type=jnp.float32)
        raw += jnp.dot(table[0, :, split:], halo, preferred_element_type=jnp.float32)
        raw = raw.reshape(-1, 2, WG, main.shape[1])
        out[...] = (raw * inv).astype(jnp.bfloat16)


def band(record, core, lo, hi, inv=None):
    channels = record.shape[1]
    table = tables(lo, hi)
    rows = table.shape[1]
    first = inv is None
    spectra_spec = pl.BlockSpec((hi - lo, 2, WG, channels), lambda i, c: (0, 0, i, 0))
    inv_spec = pl.BlockSpec((WG, channels), lambda i, c: (i, 0))
    spectra = jax.ShapeDtypeStruct((hi - lo, 2, WIN, channels), jnp.bfloat16)
    in_specs = [
        pl.BlockSpec((WG * HOP, channels), lambda i, c: (i, 0)),
        pl.BlockSpec((HOP, channels), lambda i, c: ((i + 1) * WG, 0)),
        pl.BlockSpec((1, rows, table.shape[2]), lambda i, c: (c[0], 0, 0)),
        pl.BlockSpec((1, rows, table.shape[2]), lambda i, c: (1 - c[0], 0, 0)),
    ]
    out_specs, out_shape = [spectra_spec] * 2, [spectra] * 2
    args = [core, record, record, table, table]
    if first:
        out_specs.append(inv_spec)
        out_shape.append(jax.ShapeDtypeStruct((WIN, channels), jnp.float32))
    else:
        in_specs.append(inv_spec)
        args.append(inv)
    return pl.pallas_call(
        functools.partial(band_kernel, first),
        grid_spec=pltpu.PrefetchScalarGridSpec(
            num_scalar_prefetch=1,
            grid=(WIN // WG,),
            in_specs=in_specs,
            out_specs=out_specs,
        ),
        out_shape=out_shape,
        name="band_first" if first else "band_rest",
        compiler_params=pltpu.CompilerParams(vmem_limit_bytes=48 * 2**20),
        cost_estimate=pl.CostEstimate(
            flops=4 * rows * WIN // WG * table.shape[2] * channels,
            bytes_accessed=2 * record.size,
            transcendentals=0,
        ),
    )(*args)


def route(plan, moves):
    arrays = []

    def place(a):
        for i, b in enumerate(arrays):
            if b is a:
                return i
        arrays.append(a)
        return len(arrays) - 1

    laid = []
    for step, column, pieces, singles in moves:
        laid.append((step, column, [[place(a) for a in group] for group in pieces], [place(a) for a in singles]))
    shape = moves[0][2][0][0].shape[1:]

    def kernel(plan_ref, *refs):
        ins, outs, sems = refs[: len(arrays)], refs[len(arrays) : -1], refs[-1]
        for m, (step, column, pieces, singles) in enumerate(laid):
            which, row = plan_ref[step, column], plan_ref[step, column + 1]
            for g, group in enumerate(pieces):
                base = 0
                for a in group:
                    count = ins[a].shape[0]

                    @pl.when((which == g) & (row >= base) & (row < base + count))
                    def _(a=a, base=base, m=m, row=row, count=count):
                        index = jnp.clip(row - base, 0, count - 1)
                        pltpu.make_async_copy(ins[a].at[index], outs[m], sems.at[m]).start()

                    base += count
            for g, a in enumerate(singles):

                @pl.when(which == len(pieces) + g)
                def _(a=a, m=m):
                    pltpu.make_async_copy(ins[a], outs[m], sems.at[m]).start()

        for m in range(len(laid)):
            pltpu.make_async_copy(outs[m], outs[m], sems.at[m]).wait()

    size = math.prod(shape)
    return pl.pallas_call(
        kernel,
        in_specs=[pl.BlockSpec(memory_space=pltpu.SMEM)] + [pl.BlockSpec(memory_space=HBM)] * len(arrays),
        out_specs=[pl.BlockSpec(memory_space=HBM)] * len(laid),
        out_shape=[jax.ShapeDtypeStruct(shape, jnp.bfloat16)] * len(laid),
        scratch_shapes=[pltpu.SemaphoreType.DMA((len(laid),))],
        name="route",
        cost_estimate=pl.CostEstimate(flops=0, bytes_accessed=4 * size * len(laid), transcendentals=0),
    )(plan, *arrays)


def transposed_dot(a, b):
    return lax.dot_general(a, b, (((0,), (0,)), ((), ())), preferred_element_type=jnp.float32)


def cross_kernel(core_ref, mine_ref, other_ref, near_ref, far_ref, *refs):
    out_ref = refs[-1]

    def emit(own, paired):
        p, q, pj, qj = own[0, 0], own[0, 1], paired[0], paired[1]
        scale = 1.0 / math.sqrt(WIN)
        real = transposed_dot(p, pj) + transposed_dot(q, qj)
        imag = transposed_dot(q, pj) - transposed_dot(p, qj)
        out_ref[0, 0, 0] = (real * scale).astype(jnp.bfloat16)
        out_ref[0, 1, 0] = (imag * scale).astype(jnp.bfloat16)

    @pl.when(pl.program_id(0) == 0)
    def _():
        emit(mine_ref, near_ref)

    @pl.when(pl.program_id(0) == 1)
    def _():
        emit(other_ref, far_ref)


def cross(out, core, mine, other, row, near, far, round_index, bin_index):
    channels = near.shape[-1]
    own_spec = pl.BlockSpec((1, 2, WIN, channels), lambda g, c: (row, 0, 0, 0))
    paired_spec = pl.BlockSpec((2, WIN, channels), lambda g, c: (0, 0, 0))
    out_spec = pl.BlockSpec(
        (1, 2, 1, channels, channels),
        lambda g, c: (round_index, 0, ((c[0] + g) % CORES) * HALF + bin_index, 0, 0),
    )
    in_specs = [own_spec, own_spec, paired_spec, paired_spec]
    args = [core, mine, other, near, far]
    aliases = {}
    if out is not None:
        in_specs.append(pl.BlockSpec(memory_space=HBM))
        args.append(out)
        aliases = {len(args) - 1: 0}
    return pl.pallas_call(
        cross_kernel,
        grid_spec=pltpu.PrefetchScalarGridSpec(
            num_scalar_prefetch=1, grid=(CORES,), in_specs=in_specs, out_specs=out_spec
        ),
        out_shape=jax.ShapeDtypeStruct((ROUNDS, 2, NB, channels, channels), jnp.bfloat16),
        input_output_aliases=aliases,
        name="cross",
        compiler_params=pltpu.CompilerParams(vmem_limit_bytes=32 * 2**20),
        cost_estimate=pl.CostEstimate(
            flops=16 * WIN * channels * channels,
            bytes_accessed=12 * WIN * channels * 2,
            transcendentals=0,
        ),
    )(*args)


def body(record, owner_order):
    groups, members = lax.axis_size("blk"), lax.axis_size("grp")
    chips = members // CORES
    group, member = lax.axis_index("blk"), lax.axis_index("grp")
    chip, core = member // CORES, member % CORES
    core_arg = core.reshape(1).astype(jnp.int32)

    up = [(m, m + CORES) for m in range(members - CORES)]
    down = [(m + CORES, m) for m in range(members - CORES)]
    swap = [(m, m ^ 1) for m in range(members)]

    order = np.array(ORDER)
    asked = jnp.stack([owner_order[r, (group + r) % groups] for r in ORDER])
    chunks = ROUNDS * HALF
    steps = chunks + LAG * (chips - 2)
    links = chips - 1

    def source_of(k):
        k = jnp.clip(k, 0, chunks - 1)
        owner = jnp.take(asked, k // HALF)
        return owner // CORES, (owner % CORES != core).astype(jnp.int32), k % HALF

    t = jnp.arange(steps, dtype=jnp.int32)
    columns = []
    for hop in (chip, chips - 1 - chip):
        home, held, row = source_of(t - LAG * hop)
        columns += [jnp.where((home == chip) | (t < LAG), held, 2), row]
    home, held, row = source_of(t)
    arrived = jnp.where(home < chip, 2 + chip - 1, 2 + links + chips - 2 - chip)
    columns += [jnp.where(home == chip, held, arrived), row]
    plan = jnp.stack(columns, axis=1).astype(jnp.int32)

    mine_a, other_a, inv = band(record, core_arg, 0, FIRST)
    twin_a = lax.ppermute(other_a, "grp", swap)
    mine_b, other_b = band(record, core_arg, FIRST, HALF, inv)
    twin_b = lax.ppermute(other_b, "grp", swap)

    from_below, from_above = [], []
    out = None
    for step in range(steps + 1):
        if step < FIRST:
            held = [[mine_a], [twin_a]]
        else:
            held = [[mine_a, mine_b], [twin_a, twin_b]]
        moves = []
        if step < steps:
            below = [from_below[step - LAG]] if step >= LAG else []
            above = [from_above[step - LAG]] if step >= LAG else []
            moves += [(step, 0, held, below), (step, 2, held, above)]
        k = step - LAG * (chips - 2) - 1
        if k >= 0:
            candidates = [from_below[k + LAG * j] for j in range(links)]
            candidates += [from_above[k + LAG * j] for j in range(links)]
            moves.append((k, 4, held, candidates))
        sent = route(plan, moves)
        if step < steps:
            from_below.append(lax.ppermute(sent[0], "grp", up))
            from_above.append(lax.ppermute(sent[1], "grp", down))
        if k >= 0:
            round_index, bin_index = ORDER[k // HALF], k % HALF
            near = sent[-1]
            if round_index:
                pairs = [(g, (g + round_index) % groups) for g in range(groups)]
                near = lax.ppermute(near, "blk", pairs)
            far = lax.ppermute(near, "grp", swap)
            own = (mine_a, other_a, bin_index) if bin_index < FIRST else (mine_b, other_b, bin_index - FIRST)
            out = cross(out, core_arg, *own, near, far, round_index, bin_index)
    return out


def solution(mesh):
    return jax.shard_map(
        body,
        mesh=mesh,
        in_specs=(P(None, ("blk", "grp")), P()),
        out_specs=P(None, None, None, ("blk", "grp"), None),
        check_vma=False,
    )
```

time: 719 us -> 1420 us (1.97)
  Pallas kernels: 0 us -> 1000 us
  waiting for transfers between devices: 590 us -> 201 us
  starting transfers between devices: 3.73 us -> 171 us
  matrix products: 42.6 us -> 0 us
  other arithmetic: 37.4 us -> 5.16 us
  between operations: 16.1 us -> 1.63 us
    pallas_call x0 -> x71, Pallas kernels: none -> 1000 us  [the longest x37 905 us: route(): pl.pallas_call(kernel, in_specs=[pl.BlockSpec(memory_space=pltpu.SMEM)] +...]
    psum x1 -> x0, waiting for transfers between devices: 321 us -> none  [broadcast(): return lax.psum(kept, axis)]
    ppermute x3 -> x130, starting transfers between devices: 3.73 us -> 171 us  [the longest x36 91.4 us: body(): from_below.append(lax.ppermute(sent[0], 'grp', up))]
    ppermute x3 -> x130, waiting for transfers between devices: 269 us -> 201 us  [the longest x36 123 us: body(): from_above.append(lax.ppermute(sent[1], 'grp', down))]
    dot_general x18 -> x0, matrix products: 42.6 us -> none  [the longest x4 10.3 us: cross_stack(): jnp.einsum('wfi,wfj->fij', real_own, imag_other, preferred_element_type=j...]
    unnamed x20 -> x202, local copies, waits for them, and re-layouts: 9.96 us -> 32 us
    slice x7 -> x0, local copies, waits for them, and re-layouts: 17.8 us -> none  [the longest x3 11.9 us: cross_stack(): real_own, imag_own = (own[:, :NB], own[:, NB:])]
    select_n x4 -> x2, other arithmetic: 17.6 us -> 0.03 us  [source_of(): return (owner // CORES, (owner % CORES != core).astype(jnp.int32), k % HALF)]
  transfers between devices with their start and end apart: 4 -> 130, of which waited for: 4 -> 59; matrix products, arithmetic and copies ran while one was open for 2% -> 0% of each run, Pallas kernels for 0% -> 32%
where the time goes in v1:
time: 1420 us; the launch traced here: 1410 us
  Pallas kernels  1000 us (70%)
  waiting for transfers between devices  201 us (14%)
  starting transfers between devices  171 us (12%)
  local copies, waits for them, and re-layouts  33.4 us (2%)
    pallas_call x37, Pallas kernels, route(): pl.pallas_call(kernel, in_specs=[pl.BlockSpec(memory_space=pltpu.SMEM)] +...  905 us
    ppermute x36, waiting for transfers between devices, body(): from_above.append(lax.ppermute(sent[1], 'grp', down))  123 us
    ppermute x36, starting transfers between devices, body(): from_below.append(lax.ppermute(sent[0], 'grp', up))  91.4 us
    ppermute x36, waiting for transfers between devices, body(): from_below.append(lax.ppermute(sent[0], 'grp', up))  77.2 us
    pallas_call x32, Pallas kernels, cross(): pl.pallas_call(cross_kernel, grid_spec=pltpu.PrefetchScalarGridSpec(num_s...  72.2 us
    ppermute x36, starting transfers between devices, body(): from_above.append(lax.ppermute(sent[1], 'grp', down))  46.6 us
    unnamed x202, local copies, waits for them, and re-layouts  32 us
  transfers between devices with their start and end apart: 130, of which 59 were waited for; matrix products, arithmetic and copies ran while one was open for 0% of the time, Pallas kernels for 32%

profile of v1, /device:TPU:0, one launch (start us, length us, event | category | flops | bytes accessed | tf_op | source)
XLA Modules:
  0.0 1413.6 jit_solution(14031050373194768963)
XLA Ops:
  1.0 11.9 band_first.1
  13.8 12.8 band_rest.1
  35.7 18.0 %route.39 = (bf16[2,256,256]{2,1,0:T(8,128)(2,1)}, bf16[2,256,256]{2,1,0:T(8,128)(2,1)}) custom-call(s32[36,6]{1,0:T(8,128)} %copy.75.plan_ref, bf16[2,2,256,256]{3,2,1,0:T(8,128)(2,1)} %copy-done.4, bf16[2,2,256,256]{3,2,1,0:T(8,128)(2,1)} %copy-done.37), custom_call_target="tpu_custom_call" | custom-call | bytes 1048576 | tf_op jit(solution)/shard_map/route/pallas_call | solution.py:156
  53.7 5.0 collective-permute-start.6
  60.0 18.0 %route.37 = (bf16[2,256,256]{2,1,0:T(8,128)(2,1)}, bf16[2,256,256]{2,1,0:T(8,128)(2,1)}) custom-call(s32[36,6]{1,0:T(8,128)} %copy.75.plan_ref, bf16[2,2,256,256]{3,2,1,0:T(8,128)(2,1)} %copy-done.4, bf16[2,2,256,256]{3,2,1,0:T(8,128)(2,1)} %copy-done.37), custom_call_target="tpu_custom_call" | custom-call | bytes 1048576 | tf_op jit(solution)/shard_map/route/pallas_call | solution.py:156
  78.0 4.6 collective-permute-start.2
  84.7 18.0 %route.40 = (bf16[2,256,256]{2,1,0:T(8,128)(2,1)}, bf16[2,256,256]{2,1,0:T(8,128)(2,1)}) custom-call(s32[36,6]{1,0:T(8,128)} %copy.75.plan_ref, bf16[2,2,256,256]{3,2,1,0:T(8,128)(2,1)} %copy-done.4, bf16[6,2,256,256]{3,2,1,0:T(8,128)(2,1)} %copy-done, bf16[2,2,256,256]{3,2,1,0:T(8,128)(2,1)} %copy-done.37, ...), custom_call_target="tpu_custom_call" | custom-call | bytes 1048576 | tf_op jit(solution)/shard_map/route/pallas_call | solution.py:156
  102.7 4.6 collective-permute-start.8
  110.0 18.0 %route.38 = (bf16[2,256,256]{2,1,0:T(8,128)(2,1)}, bf16[2,256,256]{2,1,0:T(8,128)(2,1)}) custom-call(s32[36,6]{1,0:T(8,128)} %copy.75.plan_ref, bf16[2,2,256,256]{3,2,1,0:T(8,128)(2,1)} %copy-done.4, bf16[6,2,256,256]{3,2,1,0:T(8,128)(2,1)} %copy-done, bf16[2,2,256,256]{3,2,1,0:T(8,128)(2,1)} %copy-done.37, ...), custom_call_target="tpu_custom_call" | custom-call | bytes 1048576 | tf_op jit(solution)/shard_map/route/pallas_call | solution.py:156
  128.0 4.6 collective-permute-start.4
  135.3 18.0 %route.41 = (bf16[2,256,256]{2,1,0:T(8,128)(2,1)}, bf16[2,256,256]{2,1,0:T(8,128)(2,1)}) custom-call(s32[36,6]{1,0:T(8,128)} %copy.75.plan_ref, bf16[2,2,256,256]{3,2,1,0:T(8,128)(2,1)} %copy-done.4, bf16[6,2,256,256]{3,2,1,0:T(8,128)(2,1)} %copy-done, bf16[2,2,256,256]{3,2,1,0:T(8,128)(2,1)} %copy-done.37, ...), custom_call_target="tpu_custom_call" | custom-call | bytes 1048576 | tf_op jit(solution)/shard_map/route/pallas_call | solution.py:156
  153.3 4.6 collective-permute-start.10
  167.1 26.0 %route.42 = (bf16[2,256,256]{2,1,0:T(8,128)(2,1)}, bf16[2,256,256]{2,1,0:T(8,128)(2,1)}, bf16[2,256,256]{2,1,0:T(8,128)(2,1)}) custom-call(s32[36,6]{1,0:T(8,128)} %copy.75.plan_ref, bf16[2,2,256,256]{3,2,1,0:T(8,128)(2,1)} %copy-done.4, bf16[6,2,256,256]{3,2,1,0:T(8,128)(2,1)} %copy-done, bf16[2,2,256,256]{3,2,1,0:T(8,128)(2,1)} %copy-done.37, ...), custom_call_target="tpu_custom_call" | custom-call | bytes 1572864 | tf_op jit(solution)/shard_map/route/pallas_call | solution.py:156
  205.7 26.0 %route.43 = (bf16[2,256,256]{2,1,0:T(8,128)(2,1)}, bf16[2,256,256]{2,1,0:T(8,128)(2,1)}, bf16[2,256,256]{2,1,0:T(8,128)(2,1)}) custom-call(s32[36,6]{1,0:T(8,128)} %copy.75.plan_ref, bf16[2,2,256,256]{3,2,1,0:T(8,128)(2,1)} %copy-done.4, bf16[6,2,256,256]{3,2,1,0:T(8,128)(2,1)} %copy-done, bf16[2,2,256,256]{3,2,1,0:T(8,128)(2,1)} %copy-done.37, ...), custom_call_target="tpu_custom_call" | custom-call | bytes 1572864 | tf_op jit(solution)/shard_map/route/pallas_call | solution.py:156
  239.3 4.3 collective-permute-done.15.refs_11_.refs_5_.refs_10_.refs_9_
  244.4 26.0 %route.44 = (bf16[2,256,256]{2,1,0:T(8,128)(2,1)}, bf16[2,256,256]{2,1,0:T(8,128)(2,1)}, bf16[2,256,256]{2,1,0:T(8,128)(2,1)}) custom-call(s32[36,6]{1,0:T(8,128)} %copy.75.plan_ref, bf16[2,2,256,256]{3,2,1,0:T(8,128)(2,1)} %copy-done.4, bf16[6,2,256,256]{3,2,1,0:T(8,128)(2,1)} %copy-done, bf16[2,2,256,256]{3,2,1,0:T(8,128)(2,1)} %copy-done.37, ...), custom_call_target="tpu_custom_call" | custom-call | bytes 1572864 | tf_op jit(solution)/shard_map/route/pallas_call | solution.py:156
  281.4 25.9 %route.45 = (bf16[2,256,256]{2,1,0:T(8,128)(2,1)}, bf16[2,256,256]{2,1,0:T(8,128)(2,1)}, bf16[2,256,256]{2,1,0:T(8,128)(2,1)}) custom-call(s32[36,6]{1,0:T(8,128)} %copy.75.plan_ref, bf16[2,2,256,256]{3,2,1,0:T(8,128)(2,1)} %copy-done.4, bf16[6,2,256,256]{3,2,1,0:T(8,128)(2,1)} %copy-done, bf16[2,2,256,256]{3,2,1,0:T(8,128)(2,1)} %copy-done.37, ...), custom_call_target="tpu_custom_call" | custom-call | bytes 1572864 | tf_op jit(solution)/shard_map/route/pallas_call | solution.py:156
  318.5 25.9 %route.46 = (bf16[2,256,256]{2,1,0:T(8,128)(2,1)}, bf16[2,256,256]{2,1,0:T(8,128)(2,1)}, bf16[2,256,256]{2,1,0:T(8,128)(2,1)}) custom-call(s32[36,6]{1,0:T(8,128)} %copy.75.plan_ref, bf16[2,2,256,256]{3,2,1,0:T(8,128)(2,1)} %copy-done.4, bf16[6,2,256,256]{3,2,1,0:T(8,128)(2,1)} %copy-done, bf16[2,2,256,256]{3,2,1,0:T(8,128)(2,1)} %copy-done.37, ...), custom_call_target="tpu_custom_call" | custom-call | bytes 1572864 | tf_op jit(solution)/shard_map/route/pallas_call | solution.py:156
  355.6 26.0 %route.47 = (bf16[2,256,256]{2,1,0:T(8,128)(2,1)}, bf16[2,256,256]{2,1,0:T(8,128)(2,1)}, bf16[2,256,256]{2,1,0:T(8,128)(2,1)}) custom-call(s32[36,6]{1,0:T(8,128)} %copy.75.plan_ref, bf16[2,2,256,256]{3,2,1,0:T(8,128)(2,1)} %copy-done.4, bf16[6,2,256,256]{3,2,1,0:T(8,128)(2,1)} %copy-done, bf16[2,2,256,256]{3,2,1,0:T(8,128)(2,1)} %copy-done.37, ...), custom_call_target="tpu_custom_call" | custom-call | bytes 1572864 | tf_op jit(solution)/shard_map/route/pallas_call | solution.py:156
  392.7 26.0 %route.48 = (bf16[2,256,256]{2,1,0:T(8,128)(2,1)}, bf16[2,256,256]{2,1,0:T(8,128)(2,1)}, bf16[2,256,256]{2,1,0:T(8,128)(2,1)}) custom-call(s32[36,6]{1,0:T(8,128)} %copy.75.plan_ref, bf16[2,2,256,256]{3,2,1,0:T(8,128)(2,1)} %copy-done.4, bf16[6,2,256,256]{3,2,1,0:T(8,128)(2,1)} %copy-done, bf16[2,2,256,256]{3,2,1,0:T(8,128)(2,1)} %copy-done.37, ...), custom_call_target="tpu_custom_call" | custom-call | bytes 1572864 | tf_op jit(solution)/shard_map/route/pallas_call | solution.py:156
  429.8 26.0 %route.49 = (bf16[2,256,256]{2,1,0:T(8,128)(2,1)}, bf16[2,256,256]{2,1,0:T(8,128)(2,1)}, bf16[2,256,256]{2,1,0:T(8,128)(2,1)}) custom-call(s32[36,6]{1,0:T(8,128)} %copy.75.plan_ref, bf16[2,2,256,256]{3,2,1,0:T(8,128)(2,1)} %copy-done.4, bf16[6,2,256,256]{3,2,1,0:T(8,128)(2,1)} %copy-done, bf16[2,2,256,256]{3,2,1,0:T(8,128)(2,1)} %copy-done.37, ...), custom_call_target="tpu_custom_call" | custom-call | bytes 1572864 | tf_op jit(solution)/shard_map/route/pallas_call | solution.py:156
  466.8 26.0 %route.50 = (bf16[2,256,256]{2,1,0:T(8,128)(2,1)}, bf16[2,256,256]{2,1,0:T(8,128)(2,1)}, bf16[2,256,256]{2,1,0:T(8,128)(2,1)}) custom-call(s32[36,6]{1,0:T(8,128)} %copy.75.plan_ref, bf16[2,2,256,256]{3,2,1,0:T(8,128)(2,1)} %copy-done.4, bf16[6,2,256,256]{3,2,1,0:T(8,128)(2,1)} %copy-done, bf16[2,2,256,256]{3,2,1,0:T(8,128)(2,1)} %copy-done.37, ...), custom_call_target="tpu_custom_call" | custom-call | bytes 1572864 | tf_op jit(solution)/shard_map/route/pallas_call | solution.py:156
  503.9 26.0 %route.51 = (bf16[2,256,256]{2,1,0:T(8,128)(2,1)}, bf16[2,256,256]{2,1,0:T(8,128)(2,1)}, bf16[2,256,256]{2,1,0:T(8,128)(2,1)}) custom-call(s32[36,6]{1,0:T(8,128)} %copy.75.plan_ref, bf16[2,2,256,256]{3,2,1,0:T(8,128)(2,1)} %copy-done.4, bf16[6,2,256,256]{3,2,1,0:T(8,128)(2,1)} %copy-done, bf16[2,2,256,256]{3,2,1,0:T(8,128)(2,1)} %copy-done.37, ...), custom_call_target="tpu_custom_call" | custom-call | bytes 1572864 | tf_op jit(solution)/shard_map/route/pallas_call | solution.py:156
  541.0 26.0 %route.52 = (bf16[2,256,256]{2,1,0:T(8,128)(2,1)}, bf16[2,256,256]{2,1,0:T(8,128)(2,1)}, bf16[2,256,256]{2,1,0:T(8,128)(2,1)}) custom-call(s32[36,6]{1,0:T(8,128)} %copy.75.plan_ref, bf16[2,2,256,256]{3,2,1,0:T(8,128)(2,1)} %copy-done.4, bf16[6,2,256,256]{3,2,1,0:T(8,128)(2,1)} %copy-done, bf16[2,2,256,256]{3,2,1,0:T(8,128)(2,1)} %copy-done.37, ...), custom_call_target="tpu_custom_call" | custom-call | bytes 1572864 | tf_op jit(solution)/shard_map/route/pallas_call | solution.py:156
  578.0 26.0 %route.53 = (bf16[2,256,256]{2,1,0:T(8,128)(2,1)}, bf16[2,256,256]{2,1,0:T(8,128)(2,1)}, bf16[2,256,256]{2,1,0:T(8,128)(2,1)}) custom-call(s32[36,6]{1,0:T(8,128)} %copy.75.plan_ref, bf16[2,2,256,256]{3,2,1,0:T(8,128)(2,1)} %copy-done.4, bf16[6,2,256,256]{3,2,1,0:T(8,128)(2,1)} %copy-done, bf16[2,2,256,256]{3,2,1,0:T(8,128)(2,1)} %copy-done.37, ...), custom_call_target="tpu_custom_call" | custom-call | bytes 1572864 | tf_op jit(solution)/shard_map/route/pallas_call | solution.py:156
  615.1 26.0 %route.54 = (bf16[2,256,256]{2,1,0:T(8,128)(2,1)}, bf16[2,256,256]{2,1,0:T(8,128)(2,1)}, bf16[2,256,256]{2,1,0:T(8,128)(2,1)}) custom-call(s32[36,6]{1,0:T(8,128)} %copy.75.plan_ref, bf16[2,2,256,256]{3,2,1,0:T(8,128)(2,1)} %copy-done.4, bf16[6,2,256,256]{3,2,1,0:T(8,128)(2,1)} %copy-done, bf16[2,2,256,256]{3,2,1,0:T(8,128)(2,1)} %copy-done.37, ...), custom_call_target="tpu_custom_call" | custom-call | bytes 1572864 | tf_op jit(solution)/shard_map/route/pallas_call | solution.py:156
  652.2 26.0 %route.55 = (bf16[2,256,256]{2,1,0:T(8,128)(2,1)}, bf16[2,256,256]{2,1,0:T(8,128)(2,1)}, bf16[2,256,256]{2,1,0:T(8,128)(2,1)}) custom-call(s32[36,6]{1,0:T(8,128)} %copy.75.plan_ref, bf16[2,2,256,256]{3,2,1,0:T(8,128)(2,1)} %copy-done.4, bf16[6,2,256,256]{3,2,1,0:T(8,128)(2,1)} %copy-done, bf16[2,2,256,256]{3,2,1,0:T(8,128)(2,1)} %copy-done.37, ...), custom_call_target="tpu_custom_call" | custom-call | bytes 1572864 | tf_op jit(solution)/shard_map/route/pallas_call | solution.py:156
  689.3 26.0 %route.56 = (bf16[2,256,256]{2,1,0:T(8,128)(2,1)}, bf16[2,256,256]{2,1,0:T(8,128)(2,1)}, bf16[2,256,256]{2,1,0:T(8,128)(2,1)}) custom-call(s32[36,6]{1,0:T(8,128)} %copy.75.plan_ref, bf16[2,2,256,256]{3,2,1,0:T(8,128)(2,1)} %copy-done.4, bf16[6,2,256,256]{3,2,1,0:T(8,128)(2,1)} %copy-done, bf16[2,2,256,256]{3,2,1,0:T(8,128)(2,1)} %copy-done.37, ...), custom_call_target="tpu_custom_call" | custom-call | bytes 1572864 | tf_op jit(solution)/shard_map/route/pallas_call | solution.py:156
  726.5 26.0 %route.57 = (bf16[2,256,256]{2,1,0:T(8,128)(2,1)}, bf16[2,256,256]{2,1,0:T(8,128)(2,1)}, bf16[2,256,256]{2,1,0:T(8,128)(2,1)}) custom-call(s32[36,6]{1,0:T(8,128)} %copy.75.plan_ref, bf16[2,2,256,256]{3,2,1,0:T(8,128)(2,1)} %copy-done.4, bf16[6,2,256,256]{3,2,1,0:T(8,128)(2,1)} %copy-done, bf16[2,2,256,256]{3,2,1,0:T(8,128)(2,1)} %copy-done.37, ...), custom_call_target="tpu_custom_call" | custom-call | bytes 1572864 | tf_op jit(solution)/shard_map/route/pallas_call | solution.py:156
  763.6 26.0 %route.58 = (bf16[2,256,256]{2,1,0:T(8,128)(2,1)}, bf16[2,256,256]{2,1,0:T(8,128)(2,1)}, bf16[2,256,256]{2,1,0:T(8,128)(2,1)}) custom-call(s32[36,6]{1,0:T(8,128)} %copy.75.plan_ref, bf16[2,2,256,256]{3,2,1,0:T(8,128)(2,1)} %copy-done.4, bf16[6,2,256,256]{3,2,1,0:T(8,128)(2,1)} %copy-done, bf16[2,2,256,256]{3,2,1,0:T(8,128)(2,1)} %copy-done.37, ...), custom_call_target="tpu_custom_call" | custom-call | bytes 1572864 | tf_op jit(solution)/shard_map/route/pallas_call | solution.py:156
  800.6 26.0 %route.59 = (bf16[2,256,256]{2,1,0:T(8,128)(2,1)}, bf16[2,256,256]{2,1,0:T(8,128)(2,1)}, bf16[2,256,256]{2,1,0:T(8,128)(2,1)}) custom-call(s32[36,6]{1,0:T(8,128)} %copy.75.plan_ref, bf16[2,2,256,256]{3,2,1,0:T(8,128)(2,1)} %copy-done.4, bf16[6,2,256,256]{3,2,1,0:T(8,128)(2,1)} %copy-done, bf16[2,2,256,256]{3,2,1,0:T(8,128)(2,1)} %copy-done.37, ...), custom_call_target="tpu_custom_call" | custom-call | bytes 1572864 | tf_op jit(solution)/shard_map/route/pallas_call | solution.py:156
  837.7 26.0 %route.60 = (bf16[2,256,256]{2,1,0:T(8,128)(2,1)}, bf16[2,256,256]{2,1,0:T(8,128)(2,1)}, bf16[2,256,256]{2,1,0:T(8,128)(2,1)}) custom-call(s32[36,6]{1,0:T(8,128)} %copy.75.plan_ref, bf16[2,2,256,256]{3,2,1,0:T(8,128)(2,1)} %copy-done.4, bf16[6,2,256,256]{3,2,1,0:T(8,128)(2,1)} %copy-done, bf16[2,2,256,256]{3,2,1,0:T(8,128)(2,1)} %copy-done.37, ...), custom_call_target="tpu_custom_call" | custom-call | bytes 1572864 | tf_op jit(solution)/shard_map/route/pallas_call | solution.py:156
  874.8 26.0 %route.61 = (bf16[2,256,256]{2,1,0:T(8,128)(2,1)}, bf16[2,256,256]{2,1,0:T(8,128)(2,1)}, bf16[2,256,256]{2,1,0:T(8,128)(2,1)}) custom-call(s32[36,6]{1,0:T(8,128)} %copy.75.plan_ref, bf16[2,2,256,256]{3,2,1,0:T(8,128)(2,1)} %copy-done.4, bf16[6,2,256,256]{3,2,1,0:T(8,128)(2,1)} %copy-done, bf16[2,2,256,256]{3,2,1,0:T(8,128)(2,1)} %copy-done.37, ...), custom_call_target="tpu_custom_call" | custom-call | bytes 1572864 | tf_op jit(solution)/shard_map/route/pallas_call | solution.py:156
  911.9 26.0 %route.62 = (bf16[2,256,256]{2,1,0:T(8,128)(2,1)}, bf16[2,256,256]{2,1,0:T(8,128)(2,1)}, bf16[2,256,256]{2,1,0:T(8,128)(2,1)}) custom-call(s32[36,6]{1,0:T(8,128)} %copy.75.plan_ref, bf16[2,2,256,256]{3,2,1,0:T(8,128)(2,1)} %copy-done.4, bf16[6,2,256,256]{3,2,1,0:T(8,128)(2,1)} %copy-done, bf16[2,2,256,256]{3,2,1,0:T(8,128)(2,1)} %copy-done.37, ...), custom_call_target="tpu_custom_call" | custom-call | bytes 1572864 | tf_op jit(solution)/shard_map/route/pallas_call | solution.py:156
  948.9 26.0 %route.63 = (bf16[2,256,256]{2,1,0:T(8,128)(2,1)}, bf16[2,256,256]{2,1,0:T(8,128)(2,1)}, bf16[2,256,256]{2,1,0:T(8,128)(2,1)}) custom-call(s32[36,6]{1,0:T(8,128)} %copy.75.plan_ref, bf16[2,2,256,256]{3,2,1,0:T(8,128)(2,1)} %copy-done.4, bf16[6,2,256,256]{3,2,1,0:T(8,128)(2,1)} %copy-done, bf16[2,2,256,256]{3,2,1,0:T(8,128)(2,1)} %copy-done.37, ...), custom_call_target="tpu_custom_call" | custom-call | bytes 1572864 | tf_op jit(solution)/shard_map/route/pallas_call | solution.py:156
  986.7 26.0 %route.64 = (bf16[2,256,256]{2,1,0:T(8,128)(2,1)}, bf16[2,256,256]{2,1,0:T(8,128)(2,1)}, bf16[2,256,256]{2,1,0:T(8,128)(2,1)}) custom-call(s32[36,6]{1,0:T(8,128)} %copy.75.plan_ref, bf16[2,2,256,256]{3,2,1,0:T(8,128)(2,1)} %copy-done.4, bf16[6,2,256,256]{3,2,1,0:T(8,128)(2,1)} %copy-done, bf16[2,2,256,256]{3,2,1,0:T(8,128)(2,1)} %copy-done.37, ...), custom_call_target="tpu_custom_call" | custom-call | bytes 1572864 | tf_op jit(solution)/shard_map/route/pallas_call | solution.py:156
  1027.6 26.0 %route.65 = (bf16[2,256,256]{2,1,0:T(8,128)(2,1)}, bf16[2,256,256]{2,1,0:T(8,128)(2,1)}, bf16[2,256,256]{2,1,0:T(8,128)(2,1)}) custom-call(s32[36,6]{1,0:T(8,128)} %copy.75.plan_ref, bf16[2,2,256,256]{3,2,1,0:T(8,128)(2,1)} %copy-done.4, bf16[6,2,256,256]{3,2,1,0:T(8,128)(2,1)} %copy-done, bf16[2,2,256,256]{3,2,1,0:T(8,128)(2,1)} %copy-done.37, ...), custom_call_target="tpu_custom_call" | custom-call | bytes 1572864 | tf_op jit(solution)/shard_map/route/pallas_call | solution.py:156
  1061.2 4.9 collective-permute-done.59.refs_11_.refs_5_.refs_10_.refs_9_
  1066.7 26.0 %route.66 = (bf16[2,256,256]{2,1,0:T(8,128)(2,1)}, bf16[2,256,256]{2,1,0:T(8,128)(2,1)}, bf16[2,256,256]{2,1,0:T(8,128)(2,1)}) custom-call(s32[36,6]{1,0:T(8,128)} %copy.75.plan_ref, bf16[2,2,256,256]{3,2,1,0:T(8,128)(2,1)} %copy-done.4, bf16[6,2,256,256]{3,2,1,0:T(8,128)(2,1)} %copy-done, bf16[2,2,256,256]{3,2,1,0:T(8,128)(2,1)} %copy-done.37, ...), custom_call_target="tpu_custom_call" | custom-call | bytes 1572864 | tf_op jit(solution)/shard_map/route/pallas_call | solution.py:156
  1105.6 26.0 %route.67 = (bf16[2,256,256]{2,1,0:T(8,128)(2,1)}, bf16[2,256,256]{2,1,0:T(8,128)(2,1)}, bf16[2,256,256]{2,1,0:T(8,128)(2,1)}) custom-call(s32[36,6]{1,0:T(8,128)} %copy.75.plan_ref, bf16[2,2,256,256]{3,2,1,0:T(8,128)(2,1)} %copy-done.4, bf16[6,2,256,256]{3,2,1,0:T(8,128)(2,1)} %copy-done, bf16[2,2,256,256]{3,2,1,0:T(8,128)(2,1)} %copy-done.37, ...), custom_call_target="tpu_custom_call" | custom-call | bytes 1572864 | tf_op jit(solution)/shard_map/route/pallas_call | solution.py:156
  1142.6 26.0 %route.68 = (bf16[2,256,256]{2,1,0:T(8,128)(2,1)}, bf16[2,256,256]{2,1,0:T(8,128)(2,1)}, bf16[2,256,256]{2,1,0:T(8,128)(2,1)}) custom-call(s32[36,6]{1,0:T(8,128)} %copy.75.plan_ref, bf16[2,2,256,256]{3,2,1,0:T(8,128)(2,1)} %copy-done.4, bf16[6,2,256,256]{3,2,1,0:T(8,128)(2,1)} %copy-done, bf16[2,2,256,256]{3,2,1,0:T(8,128)(2,1)} %copy-done.37, ...), custom_call_target="tpu_custom_call" | custom-call | bytes 1572864 | tf_op jit(solution)/shard_map/route/pallas_call | solution.py:156
  1183.0 26.0 %route.69 = (bf16[2,256,256]{2,1,0:T(8,128)(2,1)}, bf16[2,256,256]{2,1,0:T(8,128)(2,1)}, bf16[2,256,256]{2,1,0:T(8,128)(2,1)}) custom-call(s32[36,6]{1,0:T(8,128)} %copy.75.plan_ref, bf16[2,2,256,256]{3,2,1,0:T(8,128)(2,1)} %copy-done.4, bf16[6,2,256,256]{3,2,1,0:T(8,128)(2,1)} %copy-done, bf16[2,2,256,256]{3,2,1,0:T(8,128)(2,1)} %copy-done.37, ...), custom_call_target="tpu_custom_call" | custom-call | bytes 1572864 | tf_op jit(solution)/shard_map/route/pallas_call | solution.py:156
  1216.2 4.5 collective-permute-done.67.refs_11_.refs_5_.refs_10_
  1220.8 26.0 %route.70 = (bf16[2,256,256]{2,1,0:T(8,128)(2,1)}, bf16[2,256,256]{2,1,0:T(8,128)(2,1)}, bf16[2,256,256]{2,1,0:T(8,128)(2,1)}) custom-call(s32[36,6]{1,0:T(8,128)} %copy.75.plan_ref, bf16[2,2,256,256]{3,2,1,0:T(8,128)(2,1)} %copy-done.4, bf16[6,2,256,256]{3,2,1,0:T(8,128)(2,1)} %copy-done, bf16[2,2,256,256]{3,2,1,0:T(8,128)(2,1)} %copy-done.37, ...), custom_call_target="tpu_custom_call" | custom-call | bytes 1572864 | tf_op jit(solution)/shard_map/route/pallas_call | solution.py:156
  1259.6 26.0 %route.71 = (bf16[2,256,256]{2,1,0:T(8,128)(2,1)}, bf16[2,256,256]{2,1,0:T(8,128)(2,1)}, bf16[2,256,256]{2,1,0:T(8,128)(2,1)}) custom-call(s32[36,6]{1,0:T(8,128)} %copy.75.plan_ref, bf16[2,2,256,256]{3,2,1,0:T(8,128)(2,1)} %copy-done.4, bf16[6,2,256,256]{3,2,1,0:T(8,128)(2,1)} %copy-done, bf16[2,2,256,256]{3,2,1,0:T(8,128)(2,1)} %copy-done.37, ...), custom_call_target="tpu_custom_call" | custom-call | bytes 1572864 | tf_op jit(solution)/shard_map/route/pallas_call | solution.py:156
  1305.1 26.0 %route.72 = (bf16[2,256,256]{2,1,0:T(8,128)(2,1)}, bf16[2,256,256]{2,1,0:T(8,128)(2,1)}, bf16[2,256,256]{2,1,0:T(8,128)(2,1)}) custom-call(s32[36,6]{1,0:T(8,128)} %copy.75.plan_ref, bf16[2,2,256,256]{3,2,1,0:T(8,128)(2,1)} %copy-done.4, bf16[6,2,256,256]{3,2,1,0:T(8,128)(2,1)} %copy-done, bf16[2,2,256,256]{3,2,1,0:T(8,128)(2,1)} %copy-done.37, ...), custom_call_target="tpu_custom_call" | custom-call | bytes 1572864 | tf_op jit(solution)/shard_map/route/pallas_call | solution.py:156
  1331.1 4.7 collective-permute-start.72
  1372.3 10.1 route.73.near_ref
  (492 shorter events, 441.0 us)
Async XLA Ops:
  27.8 56.1 %collective-permute-start.1 = (bf16[6,2,256,256]{3,2,1,0:T(8,128)(2,1)S(1)}, bf16[6,2,256,256]{3,2,1,0:T(8,128)(2,1)}, u32[]{:S(2)}, u32[]{:S(2)}) collective-permute-start(bf16[6,2,256,256]{3,2,1,0:T(8,128)(2,1)S(1)} %get-tuple-element.116.other_ref), channel_id=1, source_target_pairs={{0,1},{1,0},{2,3},{3,2},{4,5},{5,4},{6,7},{7,6},{8,9},{9,8},{10,11... | collective-permute-start | bytes 4718600 | tf_op jit(solution)/shard_map/ppermute | solution.py:258
  904.0 37.0 %collective-permute-start.128 = (bf16[2,256,256]{2,1,0:T(8,128)(2,1)S(1)}, bf16[2,256,256]{2,1,0:T(8,128)(2,1)S(1)}, u32[]{:S(2)}, u32[]{:S(2)}) collective-permute-start(bf16[2,256,256]{2,1,0:T(8,128)(2,1)S(1)} %copy-done.99), channel_id=1, source_target_pairs={{0,8},{8,16},{16,24},{24,0},{1,9},{9,17},{17,25},{25,1},{2,10},{10... | collective-permute-start | bytes 786440 | tf_op jit(solution)/shard_map/ppermute | solution.py:286
  941.1 35.9 %collective-permute-start.129 = (bf16[2,256,256]{2,1,0:T(8,128)(2,1)S(1)}, bf16[2,256,256]{2,1,0:T(8,128)(2,1)S(1)}, u32[]{:S(2)}, u32[]{:S(2)}) collective-permute-start(bf16[2,256,256]{2,1,0:T(8,128)(2,1)S(1)} %collective-permute-done.128.near_ref), channel_id=1, source_target_pairs={{0,1},{1,0},{2,3},{3,2},{4,5},{5,4},{6,7},{7,6},{8,9},{9,8},{10,11... | collective-permute-start | bytes 786440 | tf_op jit(solution)/shard_map/ppermute | solution.py:287
  941.1 37.1 %collective-permute-start.126 = (bf16[2,256,256]{2,1,0:T(8,128)(2,1)}, bf16[2,256,256]{2,1,0:T(8,128)(2,1)S(1)}, u32[]{:S(2)}, u32[]{:S(2)}) collective-permute-start(bf16[2,256,256]{2,1,0:T(8,128)(2,1)} %get-tuple-element.220), channel_id=1, source_target_pairs={{0,8},{8,16},{16,24},{24,0},{1,9},{9,17},{17,25},{25,1},{2,10},{10... | collective-permute-start | bytes 786440 | tf_op jit(solution)/shard_map/ppermute | solution.py:286
  942.7 35.7 %collective-permute-start.124 = (bf16[2,256,256]{2,1,0:T(8,128)(2,1)}, bf16[2,256,256]{2,1,0:T(8,128)(2,1)S(1)}, u32[]{:S(2)}, u32[]{:S(2)}) collective-permute-start(bf16[2,256,256]{2,1,0:T(8,128)(2,1)} %get-tuple-element.219), channel_id=1, source_target_pairs={{0,8},{8,16},{16,24},{24,0},{1,9},{9,17},{17,25},{25,1},{2,10},{10... | collective-permute-start | bytes 786440 | tf_op jit(solution)/shard_map/ppermute | solution.py:286
  944.2 34.7 %collective-permute-start.122 = (bf16[2,256,256]{2,1,0:T(8,128)(2,1)}, bf16[2,256,256]{2,1,0:T(8,128)(2,1)S(1)}, u32[]{:S(2)}, u32[]{:S(2)}) collective-permute-start(bf16[2,256,256]{2,1,0:T(8,128)(2,1)} %get-tuple-element.218), channel_id=1, source_target_pairs={{0,8},{8,16},{16,24},{24,0},{1,9},{9,17},{17,25},{25,1},{2,10},{10... | collective-permute-start | bytes 786440 | tf_op jit(solution)/shard_map/ppermute | solution.py:286
  978.3 34.4 %collective-permute-start.127 = (bf16[2,256,256]{2,1,0:T(8,128)(2,1)S(1)}, bf16[2,256,256]{2,1,0:T(8,128)(2,1)S(1)}, u32[]{:S(2)}, u32[]{:S(2)}) collective-permute-start(bf16[2,256,256]{2,1,0:T(8,128)(2,1)S(1)} %collective-permute-done.126.near_ref), channel_id=1, source_target_pairs={{0,1},{1,0},{2,3},{3,2},{4,5},{5,4},{6,7},{7,6},{8,9},{9,8},{10,11... | collective-permute-start | bytes 786440 | tf_op jit(solution)/shard_map/ppermute | solution.py:287
  978.4 37.2 %collective-permute-start.125 = (bf16[2,256,256]{2,1,0:T(8,128)(2,1)S(1)}, bf16[2,256,256]{2,1,0:T(8,128)(2,1)S(1)}, u32[]{:S(2)}, u32[]{:S(2)}) collective-permute-start(bf16[2,256,256]{2,1,0:T(8,128)(2,1)S(1)} %collective-permute-done.124.near_ref), channel_id=1, source_target_pairs={{0,1},{1,0},{2,3},{3,2},{4,5},{5,4},{6,7},{7,6},{8,9},{9,8},{10,11... | collective-permute-start | bytes 786440 | tf_op jit(solution)/shard_map/ppermute | solution.py:287
  978.9 38.0 %collective-permute-start.120 = (bf16[2,256,256]{2,1,0:T(8,128)(2,1)}, bf16[2,256,256]{2,1,0:T(8,128)(2,1)S(1)}, u32[]{:S(2)}, u32[]{:S(2)}) collective-permute-start(bf16[2,256,256]{2,1,0:T(8,128)(2,1)} %get-tuple-element.217), channel_id=1, source_target_pairs={{0,8},{8,16},{16,24},{24,0},{1,9},{9,17},{17,25},{25,1},{2,10},{10... | collective-permute-start | bytes 786440 | tf_op jit(solution)/shard_map/ppermute | solution.py:286
  982.6 34.6 %collective-permute-start.118 = (bf16[2,256,256]{2,1,0:T(8,128)(2,1)}, bf16[2,256,256]{2,1,0:T(8,128)(2,1)S(1)}, u32[]{:S(2)}, u32[]{:S(2)}) collective-permute-start(bf16[2,256,256]{2,1,0:T(8,128)(2,1)} %get-tuple-element.216), channel_id=1, source_target_pairs={{0,8},{8,16},{16,24},{24,0},{1,9},{9,17},{17,25},{25,1},{2,10},{10... | collective-permute-start | bytes 786440 | tf_op jit(solution)/shard_map/ppermute | solution.py:286
  1016.9 36.7 %collective-permute-start.121 = (bf16[2,256,256]{2,1,0:T(8,128)(2,1)S(1)}, bf16[2,256,256]{2,1,0:T(8,128)(2,1)}, u32[]{:S(2)}, u32[]{:S(2)}) collective-permute-start(bf16[2,256,256]{2,1,0:T(8,128)(2,1)S(1)} %collective-permute-done.120.near_ref), channel_id=1, source_target_pairs={{0,1},{1,0},{2,3},{3,2},{4,5},{5,4},{6,7},{7,6},{8,9},{9,8},{10,11... | collective-permute-start | bytes 786440 | tf_op jit(solution)/shard_map/ppermute | solution.py:287
  1017.2 38.6 %collective-permute-start.119 = (bf16[2,256,256]{2,1,0:T(8,128)(2,1)S(1)}, bf16[2,256,256]{2,1,0:T(8,128)(2,1)S(1)}, u32[]{:S(2)}, u32[]{:S(2)}) collective-permute-start(bf16[2,256,256]{2,1,0:T(8,128)(2,1)S(1)} %collective-permute-done.118.near_ref), channel_id=1, source_target_pairs={{0,1},{1,0},{2,3},{3,2},{4,5},{5,4},{6,7},{7,6},{8,9},{9,8},{10,11... | collective-permute-start | bytes 786440 | tf_op jit(solution)/shard_map/ppermute | solution.py:287
  1017.5 40.4 %collective-permute-start.116 = (bf16[2,256,256]{2,1,0:T(8,128)(2,1)}, bf16[2,256,256]{2,1,0:T(8,128)(2,1)}, u32[]{:S(2)}, u32[]{:S(2)}) collective-permute-start(bf16[2,256,256]{2,1,0:T(8,128)(2,1)} %get-tuple-element.215), channel_id=1, source_target_pairs={{0,8},{8,16},{16,24},{24,0},{1,9},{9,17},{17,25},{25,1},{2,10},{10... | collective-permute-start | bytes 786440 | tf_op jit(solution)/shard_map/ppermute | solution.py:286
  1021.4 36.5 %collective-permute-start.114 = (bf16[2,256,256]{2,1,0:T(8,128)(2,1)}, bf16[2,256,256]{2,1,0:T(8,128)(2,1)}, u32[]{:S(2)}, u32[]{:S(2)}) collective-permute-start(bf16[2,256,256]{2,1,0:T(8,128)(2,1)} %get-tuple-element.214), channel_id=1, source_target_pairs={{0,8},{8,16},{16,24},{24,0},{1,9},{9,17},{17,25},{25,1},{2,10},{10... | collective-permute-start | bytes 786440 | tf_op jit(solution)/shard_map/ppermute | solution.py:286
  1057.9 34.8 %collective-permute-start.117 = (bf16[2,256,256]{2,1,0:T(8,128)(2,1)}, bf16[2,256,256]{2,1,0:T(8,128)(2,1)}, u32[]{:S(2)}, u32[]{:S(2)}) collective-permute-start(bf16[2,256,256]{2,1,0:T(8,128)(2,1)} %collective-permute-done.116.near_ref), channel_id=1, source_target_pairs={{0,1},{1,0},{2,3},{3,2},{4,5},{5,4},{6,7},{7,6},{8,9},{9,8},{10,11... | collective-permute-start | bytes 786440 | tf_op jit(solution)/shard_map/ppermute | solution.py:287
  1057.9 37.2 %collective-permute-start.115 = (bf16[2,256,256]{2,1,0:T(8,128)(2,1)}, bf16[2,256,256]{2,1,0:T(8,128)(2,1)}, u32[]{:S(2)}, u32[]{:S(2)}) collective-permute-start(bf16[2,256,256]{2,1,0:T(8,128)(2,1)} %collective-permute-done.114.near_ref), channel_id=1, source_target_pairs={{0,1},{1,0},{2,3},{3,2},{4,5},{5,4},{6,7},{7,6},{8,9},{9,8},{10,11... | collective-permute-start | bytes 786440 | tf_op jit(solution)/shard_map/ppermute | solution.py:287
  1058.4 38.0 %collective-permute-start.110 = (bf16[2,256,256]{2,1,0:T(8,128)(2,1)}, bf16[2,256,256]{2,1,0:T(8,128)(2,1)}, u32[]{:S(2)}, u32[]{:S(2)}) collective-permute-start(bf16[2,256,256]{2,1,0:T(8,128)(2,1)} %get-tuple-element.212), channel_id=1, source_target_pairs={{0,24},{8,0},{16,8},{24,16},{1,25},{9,1},{17,9},{25,17},{2,26},{10... | collective-permute-start | bytes 786440 | tf_op jit(solution)/shard_map/ppermute | solution.py:286
  1060.6 35.9 %collective-permute-start.108 = (bf16[2,256,256]{2,1,0:T(8,128)(2,1)}, bf16[2,256,256]{2,1,0:T(8,128)(2,1)}, u32[]{:S(2)}, u32[]{:S(2)}) collective-permute-start(bf16[2,256,256]{2,1,0:T(8,128)(2,1)} %get-tuple-element.211), channel_id=1, source_target_pairs={{0,24},{8,0},{16,8},{24,16},{1,25},{9,1},{17,9},{25,17},{2,26},{10... | collective-permute-start | bytes 786440 | tf_op jit(solution)/shard_map/ppermute | solution.py:286
  1096.4 35.2 %collective-permute-start.111 = (bf16[2,256,256]{2,1,0:T(8,128)(2,1)}, bf16[2,256,256]{2,1,0:T(8,128)(2,1)}, u32[]{:S(2)}, u32[]{:S(2)}) collective-permute-start(bf16[2,256,256]{2,1,0:T(8,128)(2,1)} %collective-permute-done.110.near_ref), channel_id=1, source_target_pairs={{0,1},{1,0},{2,3},{3,2},{4,5},{5,4},{6,7},{7,6},{8,9},{9,8},{10,11... | collective-permute-start | bytes 786440 | tf_op jit(solution)/shard_map/ppermute | solution.py:287
  1096.5 37.3 %collective-permute-start.109 = (bf16[2,256,256]{2,1,0:T(8,128)(2,1)}, bf16[2,256,256]{2,1,0:T(8,128)(2,1)}, u32[]{:S(2)}, u32[]{:S(2)}) collective-permute-start(bf16[2,256,256]{2,1,0:T(8,128)(2,1)} %collective-permute-done.108.near_ref), channel_id=1, source_target_pairs={{0,1},{1,0},{2,3},{3,2},{4,5},{5,4},{6,7},{7,6},{8,9},{9,8},{10,11... | collective-permute-start | bytes 786440 | tf_op jit(solution)/shard_map/ppermute | solution.py:287
  1097.0 38.1 %collective-permute-start.106 = (bf16[2,256,256]{2,1,0:T(8,128)(2,1)}, bf16[2,256,256]{2,1,0:T(8,128)(2,1)}, u32[]{:S(2)}, u32[]{:S(2)}) collective-permute-start(bf16[2,256,256]{2,1,0:T(8,128)(2,1)} %get-tuple-element.210), channel_id=1, source_target_pairs={{0,24},{8,0},{16,8},{24,16},{1,25},{9,1},{17,9},{25,17},{2,26},{10... | collective-permute-start | bytes 786440 | tf_op jit(solution)/shard_map/ppermute | solution.py:286
  1100.3 34.9 %collective-permute-start.104 = (bf16[2,256,256]{2,1,0:T(8,128)(2,1)}, bf16[2,256,256]{2,1,0:T(8,128)(2,1)}, u32[]{:S(2)}, u32[]{:S(2)}) collective-permute-start(bf16[2,256,256]{2,1,0:T(8,128)(2,1)} %get-tuple-element.209), channel_id=1, source_target_pairs={{0,24},{8,0},{16,8},{24,16},{1,25},{9,1},{17,9},{25,17},{2,26},{10... | collective-permute-start | bytes 786440 | tf_op jit(solution)/shard_map/ppermute | solution.py:286
  1135.2 35.6 %collective-permute-start.105 = (bf16[2,256,256]{2,1,0:T(8,128)(2,1)}, bf16[2,256,256]{2,1,0:T(8,128)(2,1)}, u32[]{:S(2)}, u32[]{:S(2)}) collective-permute-start(bf16[2,256,256]{2,1,0:T(8,128)(2,1)} %collective-permute-done.104.near_ref), channel_id=1, source_target_pairs={{0,1},{1,0},{2,3},{3,2},{4,5},{5,4},{6,7},{7,6},{8,9},{9,8},{10,11... | collective-permute-start | bytes 786440 | tf_op jit(solution)/shard_map/ppermute | solution.py:287
  1135.7 36.6 %collective-permute-start.100 = (bf16[2,256,256]{2,1,0:T(8,128)(2,1)}, bf16[2,256,256]{2,1,0:T(8,128)(2,1)}, u32[]{:S(2)}, u32[]{:S(2)}) collective-permute-start(bf16[2,256,256]{2,1,0:T(8,128)(2,1)} %get-tuple-element.207), channel_id=1, source_target_pairs={{0,24},{8,0},{16,8},{24,16},{1,25},{9,1},{17,9},{25,17},{2,26},{10... | collective-permute-start | bytes 786440 | tf_op jit(solution)/shard_map/ppermute | solution.py:286
  1137.8 34.8 %collective-permute-start.98 = (bf16[2,256,256]{2,1,0:T(8,128)(2,1)}, bf16[2,256,256]{2,1,0:T(8,128)(2,1)}, u32[]{:S(2)}, u32[]{:S(2)}) collective-permute-start(bf16[2,256,256]{2,1,0:T(8,128)(2,1)} %get-tuple-element.206), channel_id=1, source_target_pairs={{0,24},{8,0},{16,8},{24,16},{1,25},{9,1},{17,9},{25,17},{2,26},{10... | collective-permute-start | bytes 786440 | tf_op jit(solution)/shard_map/ppermute | solution.py:286
  1172.3 36.7 %collective-permute-start.101 = (bf16[2,256,256]{2,1,0:T(8,128)(2,1)}, bf16[2,256,256]{2,1,0:T(8,128)(2,1)}, u32[]{:S(2)}, u32[]{:S(2)}) collective-permute-start(bf16[2,256,256]{2,1,0:T(8,128)(2,1)} %collective-permute-done.100.near_ref), channel_id=1, source_target_pairs={{0,1},{1,0},{2,3},{3,2},{4,5},{5,4},{6,7},{7,6},{8,9},{9,8},{10,11... | collective-permute-start | bytes 786440 | tf_op jit(solution)/shard_map/ppermute | solution.py:287
  1172.6 38.6 %collective-permute-start.99 = (bf16[2,256,256]{2,1,0:T(8,128)(2,1)}, bf16[2,256,256]{2,1,0:T(8,128)(2,1)}, u32[]{:S(2)}, u32[]{:S(2)}) collective-permute-start(bf16[2,256,256]{2,1,0:T(8,128)(2,1)} %collective-permute-done.98.near_ref), channel_id=1, source_target_pairs={{0,1},{1,0},{2,3},{3,2},{4,5},{5,4},{6,7},{7,6},{8,9},{9,8},{10,11... | collective-permute-start | bytes 786440 | tf_op jit(solution)/shard_map/ppermute | solution.py:287
  1172.9 39.6 %collective-permute-start.96 = (bf16[2,256,256]{2,1,0:T(8,128)(2,1)}, bf16[2,256,256]{2,1,0:T(8,128)(2,1)}, u32[]{:S(2)}, u32[]{:S(2)}) collective-permute-start(bf16[2,256,256]{2,1,0:T(8,128)(2,1)} %get-tuple-element.205), channel_id=1, source_target_pairs={{0,16},{8,24},{16,0},{24,8},{1,17},{9,25},{17,1},{25,9},{2,18},{10... | collective-permute-start | bytes 786440 | tf_op jit(solution)/shard_map/ppermute | solution.py:286
  1176.7 35.9 %collective-permute-start.94 = (bf16[2,256,256]{2,1,0:T(8,128)(2,1)}, bf16[2,256,256]{2,1,0:T(8,128)(2,1)}, u32[]{:S(2)}, u32[]{:S(2)}) collective-permute-start(bf16[2,256,256]{2,1,0:T(8,128)(2,1)} %get-tuple-element.204), channel_id=1, source_target_pairs={{0,16},{8,24},{16,0},{24,8},{1,17},{9,25},{17,1},{25,9},{2,18},{10... | collective-permute-start | bytes 786440 | tf_op jit(solution)/shard_map/ppermute | solution.py:286
  1212.5 34.3 %collective-permute-start.97 = (bf16[2,256,256]{2,1,0:T(8,128)(2,1)}, bf16[2,256,256]{2,1,0:T(8,128)(2,1)}, u32[]{:S(2)}, u32[]{:S(2)}) collective-permute-start(bf16[2,256,256]{2,1,0:T(8,128)(2,1)} %collective-permute-done.96.near_ref), channel_id=1, source_target_pairs={{0,1},{1,0},{2,3},{3,2},{4,5},{5,4},{6,7},{7,6},{8,9},{9,8},{10,11... | collective-permute-start | bytes 786440 | tf_op jit(solution)/shard_map/ppermute | solution.py:287
  1212.6 35.7 %collective-permute-start.95 = (bf16[2,256,256]{2,1,0:T(8,128)(2,1)}, bf16[2,256,256]{2,1,0:T(8,128)(2,1)}, u32[]{:S(2)}, u32[]{:S(2)}) collective-permute-start(bf16[2,256,256]{2,1,0:T(8,128)(2,1)} %collective-permute-done.94.near_ref), channel_id=1, source_target_pairs={{0,1},{1,0},{2,3},{3,2},{4,5},{5,4},{6,7},{7,6},{8,9},{9,8},{10,11... | collective-permute-start | bytes 786440 | tf_op jit(solution)/shard_map/ppermute | solution.py:287
  1213.1 36.5 %collective-permute-start.90 = (bf16[2,256,256]{2,1,0:T(8,128)(2,1)}, bf16[2,256,256]{2,1,0:T(8,128)(2,1)}, u32[]{:S(2)}, u32[]{:S(2)}) collective-permute-start(bf16[2,256,256]{2,1,0:T(8,128)(2,1)} %get-tuple-element.202), channel_id=1, source_target_pairs={{0,16},{8,24},{16,0},{24,8},{1,17},{9,25},{17,1},{25,9},{2,18},{10... | collective-permute-start | bytes 786440 | tf_op jit(solution)/shard_map/ppermute | solution.py:286
  1215.9 34.1 %collective-permute-start.88 = (bf16[2,256,256]{2,1,0:T(8,128)(2,1)}, bf16[2,256,256]{2,1,0:T(8,128)(2,1)}, u32[]{:S(2)}, u32[]{:S(2)}) collective-permute-start(bf16[2,256,256]{2,1,0:T(8,128)(2,1)} %get-tuple-element.201), channel_id=1, source_target_pairs={{0,16},{8,24},{16,0},{24,8},{1,17},{9,25},{17,1},{25,9},{2,18},{10... | collective-permute-start | bytes 786440 | tf_op jit(solution)/shard_map/ppermute | solution.py:286
  1249.6 36.0 %collective-permute-start.91 = (bf16[2,256,256]{2,1,0:T(8,128)(2,1)}, bf16[2,256,256]{2,1,0:T(8,128)(2,1)S(1)}, u32[]{:S(2)}, u32[]{:S(2)}) collective-permute-start(bf16[2,256,256]{2,1,0:T(8,128)(2,1)} %collective-permute-done.90.near_ref), channel_id=1, source_target_pairs={{0,1},{1,0},{2,3},{3,2},{4,5},{5,4},{6,7},{7,6},{8,9},{9,8},{10,11... | collective-permute-start | bytes 786440 | tf_op jit(solution)/shard_map/ppermute | solution.py:287
  1250.0 38.5 %collective-permute-start.89 = (bf16[2,256,256]{2,1,0:T(8,128)(2,1)}, bf16[2,256,256]{2,1,0:T(8,128)(2,1)S(1)}, u32[]{:S(2)}, u32[]{:S(2)}) collective-permute-start(bf16[2,256,256]{2,1,0:T(8,128)(2,1)} %collective-permute-done.88.near_ref), channel_id=1, source_target_pairs={{0,1},{1,0},{2,3},{3,2},{4,5},{5,4},{6,7},{7,6},{8,9},{9,8},{10,11... | collective-permute-start | bytes 786440 | tf_op jit(solution)/shard_map/ppermute | solution.py:287
  1250.2 40.3 %collective-permute-start.86 = (bf16[2,256,256]{2,1,0:T(8,128)(2,1)}, bf16[2,256,256]{2,1,0:T(8,128)(2,1)}, u32[]{:S(2)}, u32[]{:S(2)}) collective-permute-start(bf16[2,256,256]{2,1,0:T(8,128)(2,1)} %get-tuple-element.200), channel_id=1, source_target_pairs={{0,16},{8,24},{16,0},{24,8},{1,17},{9,25},{17,1},{25,9},{2,18},{10... | collective-permute-start | bytes 786440 | tf_op jit(solution)/shard_map/ppermute | solution.py:286
  1254.9 35.7 %collective-permute-start.84 = (bf16[2,256,256]{2,1,0:T(8,128)(2,1)}, bf16[2,256,256]{2,1,0:T(8,128)(2,1)}, u32[]{:S(2)}, u32[]{:S(2)}) collective-permute-start(bf16[2,256,256]{2,1,0:T(8,128)(2,1)} %get-tuple-element.199), channel_id=1, source_target_pairs={{0,16},{8,24},{16,0},{24,8},{1,17},{9,25},{17,1},{25,9},{2,18},{10... | collective-permute-start | bytes 786440 | tf_op jit(solution)/shard_map/ppermute | solution.py:286
  1290.5 40.6 %collective-permute-start.87 = (bf16[2,256,256]{2,1,0:T(8,128)(2,1)}, bf16[2,256,256]{2,1,0:T(8,128)(2,1)}, u32[]{:S(2)}, u32[]{:S(2)}) collective-permute-start(bf16[2,256,256]{2,1,0:T(8,128)(2,1)} %collective-permute-done.86.near_ref), channel_id=1, source_target_pairs={{0,1},{1,0},{2,3},{3,2},{4,5},{5,4},{6,7},{7,6},{8,9},{9,8},{10,11... | collective-permute-start | bytes 786440 | tf_op jit(solution)/shard_map/ppermute | solution.py:287
  1290.6 49.2 %collective-permute-start.85 = (bf16[2,256,256]{2,1,0:T(8,128)(2,1)}, bf16[2,256,256]{2,1,0:T(8,128)(2,1)}, u32[]{:S(2)}, u32[]{:S(2)}) collective-permute-start(bf16[2,256,256]{2,1,0:T(8,128)(2,1)} %collective-permute-done.84.near_ref), channel_id=1, source_target_pairs={{0,1},{1,0},{2,3},{3,2},{4,5},{5,4},{6,7},{7,6},{8,9},{9,8},{10,11... | collective-permute-start | bytes 786440 | tf_op jit(solution)/shard_map/ppermute | solution.py:287
  1291.1 52.5 %collective-permute-start.83 = (bf16[2,256,256]{2,1,0:T(8,128)(2,1)}, bf16[2,256,256]{2,1,0:T(8,128)(2,1)}, u32[]{:S(2)}, u32[]{:S(2)}) collective-permute-start(bf16[2,256,256]{2,1,0:T(8,128)(2,1)} %collective-permute-done.82.near_ref), channel_id=1, source_target_pairs={{0,1},{1,0},{2,3},{3,2},{4,5},{5,4},{6,7},{7,6},{8,9},{9,8},{10,11... | collective-permute-start | bytes 786440 | tf_op jit(solution)/shard_map/ppermute | solution.py:287
  1299.9 60.9 %collective-permute-start.81 = (bf16[2,256,256]{2,1,0:T(8,128)(2,1)S(1)}, bf16[2,256,256]{2,1,0:T(8,128)(2,1)}, u32[]{:S(2)}, u32[]{:S(2)}) collective-permute-start(bf16[2,256,256]{2,1,0:T(8,128)(2,1)S(1)} %copy-done.20), channel_id=1, source_target_pairs={{0,1},{1,0},{2,3},{3,2},{4,5},{5,4},{6,7},{7,6},{8,9},{9,8},{10,11... | collective-permute-start | bytes 786440 | tf_op jit(solution)/shard_map/ppermute | solution.py:287
  1302.5 61.1 %collective-permute-start.80 = (bf16[2,256,256]{2,1,0:T(8,128)(2,1)}, bf16[2,256,256]{2,1,0:T(8,128)(2,1)}, u32[]{:S(2)}, u32[]{:S(2)}) collective-permute-start(bf16[2,256,256]{2,1,0:T(8,128)(2,1)} %get-tuple-element.196.near_ref), channel_id=1, source_target_pairs={{0,1},{1,0},{2,3},{3,2},{4,5},{5,4},{6,7},{7,6},{8,9},{9,8},{10,11... | collective-permute-start | bytes 786440 | tf_op jit(solution)/shard_map/ppermute | solution.py:287
  1331.1 35.0 %collective-permute-start.72 = (bf16[2,256,256]{2,1,0:T(8,128)(2,1)}, bf16[2,256,256]{2,1,0:T(8,128)(2,1)S(1)}, u32[]{:S(2)}, u32[]{:S(2)}) collective-permute-start(bf16[2,256,256]{2,1,0:T(8,128)(2,1)} %get-tuple-element.189), channel_id=1, source_target_pairs={{0,2},{1,3},{2,4},{3,5},{4,6},{5,7},{8,10},{9,11},{10,12},{11,13},... | collective-permute-start | bytes 786440 | tf_op jit(solution)/shard_map/ppermute | solution.py:279
  1343.6 38.8 %collective-permute-start.79 = (bf16[2,256,256]{2,1,0:T(8,128)(2,1)}, bf16[2,256,256]{2,1,0:T(8,128)(2,1)}, u32[]{:S(2)}, u32[]{:S(2)}) collective-permute-start(bf16[2,256,256]{2,1,0:T(8,128)(2,1)} %get-tuple-element.195.near_ref), channel_id=1, source_target_pairs={{0,1},{1,0},{2,3},{3,2},{4,5},{5,4},{6,7},{7,6},{8,9},{9,8},{10,11... | collective-permute-start | bytes 786440 | tf_op jit(solution)/shard_map/ppermute | solution.py:287
  1360.8 41.6 %collective-permute-start.78 = (bf16[2,256,256]{2,1,0:T(8,128)(2,1)}, bf16[2,256,256]{2,1,0:T(8,128)(2,1)}, u32[]{:S(2)}, u32[]{:S(2)}) collective-permute-start(bf16[2,256,256]{2,1,0:T(8,128)(2,1)} %get-tuple-element.194.near_ref), channel_id=1, source_target_pairs={{0,1},{1,0},{2,3},{3,2},{4,5},{5,4},{6,7},{7,6},{8,9},{9,8},{10,11... | collective-permute-start | bytes 786440 | tf_op jit(solution)/shard_map/ppermute | solution.py:287
  1363.6 41.2 %collective-permute-start.77 = (bf16[2,256,256]{2,1,0:T(8,128)(2,1)}, bf16[2,256,256]{2,1,0:T(8,128)(2,1)}, u32[]{:S(2)}, u32[]{:S(2)}) collective-permute-start(bf16[2,256,256]{2,1,0:T(8,128)(2,1)} %get-tuple-element.193.near_ref), channel_id=1, source_target_pairs={{0,1},{1,0},{2,3},{3,2},{4,5},{5,4},{6,7},{7,6},{8,9},{9,8},{10,11... | collective-permute-start | bytes 786440 | tf_op jit(solution)/shard_map/ppermute | solution.py:287
  1366.2 41.1 %collective-permute-start.76 = (bf16[2,256,256]{2,1,0:T(8,128)(2,1)}, bf16[2,256,256]{2,1,0:T(8,128)(2,1)}, u32[]{:S(2)}, u32[]{:S(2)}) collective-permute-start(bf16[2,256,256]{2,1,0:T(8,128)(2,1)} %get-tuple-element.192.near_ref), channel_id=1, source_target_pairs={{0,1},{1,0},{2,3},{3,2},{4,5},{5,4},{6,7},{7,6},{8,9},{9,8},{10,11... | collective-permute-start | bytes 786440 | tf_op jit(solution)/shard_map/ppermute | solution.py:287
  1369.8 39.9 %collective-permute-start.75 = (bf16[2,256,256]{2,1,0:T(8,128)(2,1)}, bf16[2,256,256]{2,1,0:T(8,128)(2,1)}, u32[]{:S(2)}, u32[]{:S(2)}) collective-permute-start(bf16[2,256,256]{2,1,0:T(8,128)(2,1)} %get-tuple-element.191.near_ref), channel_id=1, source_target_pairs={{0,1},{1,0},{2,3},{3,2},{4,5},{5,4},{6,7},{7,6},{8,9},{9,8},{10,11... | collective-permute-start | bytes 786440 | tf_op jit(solution)/shard_map/ppermute | solution.py:287
  (183 other events, 4248.0 us)

commit v2 on v0

v2 whole, which is shorter than its diff:
```python
import functools
import math

import jax
import jax.numpy as jnp
import numpy as np
from jax import lax
from jax.experimental import pallas as pl
from jax.experimental.pallas import tpu as pltpu
from jax.sharding import PartitionSpec as P

WIN = 256
NS = 128
NB = 16
BIN_LO = 8
ROUNDS = 4
HOP = 64
WG = 16
CORES = 2
HALF = NB // CORES
FIRST = 4
GROUP = 4
GAP = 5
REST_AT = 1
LAG = 2
ORDER = ((1, 0), (2, 0), (3, 0), (1, 1), (2, 1), (3, 1), (0, 0), (0, 1))
VMEM = 8 * 2**20
SHORT = pl.CostEstimate(flops=1, bytes_accessed=1, transcendentals=0)


def band_table():
    n = np.arange(NS)
    q = BIN_LO + np.arange(NB)
    phase = ((q[:, None] * n[None, :]) % NS) * (2.0 * math.pi / NS)
    taper = 0.5 - 0.5 * np.cos(n * (2.0 * math.pi / NS))
    scale = 1.0 / math.sqrt(3.0 * NS / 8.0)
    real = taper * np.cos(phase) * scale
    imag = -taper * np.sin(phase) * scale
    return np.stack([real, imag], axis=1).astype(np.float32)


def banded(lo, hi):
    table = band_table().reshape(CORES, HALF, 2, NS)[:, lo:hi].swapaxes(0, 1)
    out = np.zeros((hi - lo, CORES, 2, WG, (WG + 1) * HOP), np.float32)
    for w in range(WG):
        out[..., w, w * HOP : w * HOP + NS] = table
    return jnp.asarray(out.reshape(-1, (WG + 1) * HOP).astype(jnp.bfloat16))


def in_hbm():
    return pl.BlockSpec(memory_space=pltpu.MemorySpace.HBM)


def token_shape():
    return jax.ShapeDtypeStruct((8, 128), jnp.int32)


def in_place():
    return pl.BlockSpec(memory_space=pl.ANY)


def half_energy(x):
    wide = x.astype(jnp.float32)
    return jnp.sum((wide * wide).reshape(-1, HOP, x.shape[-1]), axis=1)


def band_kernel(first, core_ref, main_ref, halo_ref, table, *refs):
    main, halo = main_ref[...], halo_ref[...]
    if first:
        out, inv_ref, _ = refs
        energy = half_energy(main)
        later = jnp.concatenate([energy[1:], half_energy(halo)], axis=0)
        inv = 1.0 / jnp.sqrt((energy + later) / NS + 1e-05)
        inv_ref[...] = inv
    else:
        inv_ref, _, out, _ = refs
        inv = inv_ref[...]
    split = WG * HOP
    raw = jnp.dot(table[:, :split], main, preferred_element_type=jnp.float32)
    raw += jnp.dot(table[:, split:], halo, preferred_element_type=jnp.float32)
    raw = raw.reshape(-1, CORES, 2, WG, main.shape[1])
    out[...] = (raw * inv).astype(jnp.bfloat16)


def band(core, record, lo, hi, inv=None, token=None):
    channels = record.shape[1]
    table = banded(lo, hi)
    rows = table.shape[0]
    first = inv is None
    inv_spec = pl.BlockSpec((WG, channels), lambda i: (i, 0))
    in_specs = [
        pl.BlockSpec(memory_space=pltpu.SMEM),
        pl.BlockSpec((WG * HOP, channels), lambda i: (i, 0)),
        pl.BlockSpec((HOP, channels), lambda i: ((i + 1) * WG, 0)),
        pl.BlockSpec(table.shape, lambda i: (0, 0)),
    ]
    out_specs = [pl.BlockSpec((hi - lo, CORES, 2, WG, channels), lambda i: (0, 0, 0, i, 0))]
    out_shape = [jax.ShapeDtypeStruct((hi - lo, CORES, 2, WIN, channels), jnp.bfloat16)]
    args = [core, record, record, table]
    if first:
        out_specs.append(inv_spec)
        out_shape.append(jax.ShapeDtypeStruct((WIN, channels), jnp.float32))
    else:
        in_specs += [inv_spec, in_place()]
        args += [inv, token]
    return pl.pallas_call(
        functools.partial(band_kernel, first),
        grid=(WIN // WG,),
        in_specs=in_specs,
        out_specs=out_specs + [in_place()],
        out_shape=out_shape + [token_shape()],
        name="band_first" if first else "band_rest",
        compiler_params=pltpu.CompilerParams(vmem_limit_bytes=VMEM),
        cost_estimate=pl.CostEstimate(
            flops=2 * rows * (WIN // WG) * table.shape[1] * channels, bytes_accessed=3 * record.size, transcendentals=0
        ),
    )(*args)


def turn_kernel(in_ref, _, out_ref, __):
    for part in range(2):
        out_ref[0, 0, :, part * WIN : (part + 1) * WIN] = in_ref[0, 0, part].T


def turn(spectra, token):
    count, channels = spectra.shape[0], spectra.shape[-1]
    return pl.pallas_call(
        turn_kernel,
        grid=(count, CORES),
        in_specs=[pl.BlockSpec((1, 1, 2, WIN, channels), lambda i, h: (i, h, 0, 0, 0)), in_place()],
        out_specs=[pl.BlockSpec((1, 1, channels, 2 * WIN), lambda i, h: (i, h, 0, 0)), in_place()],
        out_shape=[jax.ShapeDtypeStruct((count, CORES, channels, 2 * WIN), jnp.bfloat16), token_shape()],
        name="turn",
        compiler_params=pltpu.CompilerParams(vmem_limit_bytes=VMEM),
        cost_estimate=SHORT,
    )(spectra, token)


def place(arrays, a):
    for i, b in enumerate(arrays):
        if b is a:
            return i
    arrays.append(a)
    return len(arrays) - 1


def seat():
    member = lax.axis_index("grp")
    return lax.axis_index("blk"), member // CORES, member % CORES, lax.axis_size("grp") // CORES


def chunk_of(k):
    r, half = ORDER[k // GROUP]
    return r, half * GROUP + k % GROUP


def asked_of(orders, k):
    r, _ = chunk_of(k)
    return orders[r, lax.rem(lax.axis_index("blk") + r, lax.axis_size("blk"))]


def inject(orders, token, step, mine, twin, held):
    chips = lax.axis_size("grp") // CORES
    sent = [step - LAG * hop for hop in range(chips)]
    hops = [hop for hop in range(chips) if 0 <= sent[hop] < ROUNDS * HALF]
    arrays, slots = [], {}
    for hop in hops:
        _, row = chunk_of(sent[hop])
        slots[hop] = (place(arrays, mine[row // FIRST]), row % FIRST), (place(arrays, twin[row]), None)
    whole = twin[0].shape

    def kernel(orders_ref, *refs):
        ins, out, buffer, sem = refs[: len(arrays)], refs[-4], refs[-2], refs[-1]
        _, chip, core, _ = seat()
        seen = jnp.where(core == 0, chip, chips - 1 - chip)
        for hop in hops:
            owner = asked_of(orders_ref, sent[hop])
            here = (seen == hop) & (owner // CORES == chip)
            for (slot, row), same in zip(slots[hop], (True, False), strict=True):
                source = ins[slot] if row is None else ins[slot].at[row]

                @pl.when(here & ((owner % CORES == core) == same))
                def _(source=source):
                    load = pltpu.make_async_copy(source, buffer, sem.at[0])
                    load.start()
                    load.wait()
                    store = pltpu.make_async_copy(buffer, out, sem.at[1])
                    store.start()
                    store.wait()

    in_specs = [pl.BlockSpec(memory_space=pltpu.SMEM)] + [in_hbm()] * len(arrays) + [in_place()]
    args = [orders, *arrays, token]
    aliases = {}
    if held is not None:
        in_specs.append(in_place())
        args.append(held)
        aliases = {len(args) - 1: 0}
    return pl.pallas_call(
        kernel,
        in_specs=in_specs,
        out_specs=[in_place()] * 2,
        out_shape=[jax.ShapeDtypeStruct(whole, jnp.bfloat16), token_shape()],
        input_output_aliases=aliases,
        scratch_shapes=[pltpu.VMEM(whole, jnp.bfloat16), pltpu.SemaphoreType.DMA((2,))],
        name="inject",
        compiler_params=pltpu.CompilerParams(vmem_limit_bytes=4 * 2**20),
        cost_estimate=SHORT,
    )(*args)


def gather(orders, token, ks, held, swapped=None):
    arrays = []
    chips = lax.axis_size("grp") // CORES
    slots = {(k, j): place(arrays, held[k + LAG * j]) for k in ks for j in range(chips - 1)}
    extra = [] if swapped is None else [swapped]
    shape = held[0].shape[1:]

    def kernel(orders_ref, *refs):
        ins, out, sems = refs[: len(arrays)], refs[-3], refs[-1]
        _, chip, core, _ = seat()
        hop = jnp.where(core == 0, chip, chips - 1 - chip)
        home = asked_of(orders_ref, ks[0]) // CORES
        has = (hop >= 1) & ((home == chip) | ((core == 0) == (home < chip)))
        half = 1 - core if swapped is None else core
        lead = jnp.maximum(hop, 1) - 1
        for j in range(chips - 1):

            @pl.when((lead == j) & (has if swapped is not None else lead == j))
            def _(j=j):
                for m, k in enumerate(ks):
                    pltpu.make_async_copy(ins[slots[k, j]].at[half], out.at[m], sems.at[m]).start()

        if swapped is not None:

            @pl.when(jnp.logical_not(has))
            def _():
                for m in range(len(ks)):
                    pltpu.make_async_copy(refs[len(arrays)].at[m], out.at[m], sems.at[m]).start()

        for m in range(len(ks)):
            pltpu.make_async_copy(out.at[m], out.at[m], sems.at[m]).wait()

    return pl.pallas_call(
        kernel,
        in_specs=[pl.BlockSpec(memory_space=pltpu.SMEM)] + [in_place()] * (len(arrays) + len(extra) + 1),
        out_specs=[pl.BlockSpec(memory_space=pltpu.VMEM), in_place()],
        out_shape=[jax.ShapeDtypeStruct((len(ks), *shape), jnp.bfloat16), token_shape()],
        scratch_shapes=[pltpu.SemaphoreType.DMA((len(ks),))],
        name="collect" if swapped is None else "select",
        compiler_params=pltpu.CompilerParams(vmem_limit_bytes=8 * 2**20),
        cost_estimate=SHORT,
    )(orders, *arrays, *extra, token)


def cross_kernel(core_ref, own_ref, near_ref, far_ref, *refs):
    out_ref = refs[-2]

    def emit(paired_ref):
        own = own_ref[0, 0]
        turned = jnp.concatenate([own[:, WIN:], -own[:, :WIN]], axis=1)
        paired = paired_ref[0].reshape(2 * WIN, -1)
        scale = 1.0 / math.sqrt(WIN)
        for part, lhs in enumerate((own, turned)):
            total = jnp.dot(lhs, paired, preferred_element_type=jnp.float32)
            out_ref[0, part, 0] = (total * scale).astype(jnp.bfloat16)

    @pl.when(pl.program_id(1) == 0)
    def _():
        emit(near_ref)

    @pl.when(pl.program_id(1) == 1)
    def _():
        emit(far_ref)


def cross(out, token, core, own, near, far, round_index, first_chunk, begin, count):
    channels = near.shape[-1]
    first_chunk += begin
    row = first_chunk % own.shape[0]
    paired_spec = pl.BlockSpec((1, 2, WIN, channels), lambda i, g, c: (begin + i, 0, 0, 0))
    in_specs = [
        pl.BlockSpec((1, 1, channels, 2 * WIN), lambda i, g, c: (row + i, (c[0] + g) % CORES, 0, 0)),
        paired_spec,
        paired_spec,
        in_place(),
    ]
    out_spec = pl.BlockSpec(
        (1, 2, 1, channels, channels),
        lambda i, g, c: (round_index, 0, ((c[0] + g) % CORES) * HALF + first_chunk + i, 0, 0),
    )
    args = [core, own, near, far, token]
    aliases = {}
    if out is not None:
        in_specs.append(in_place())
        args.append(out)
        aliases = {len(args) - 1: 0}
    return pl.pallas_call(
        cross_kernel,
        grid_spec=pltpu.PrefetchScalarGridSpec(
            num_scalar_prefetch=1, grid=(count, CORES), in_specs=in_specs, out_specs=[out_spec, in_place()]
        ),
        out_shape=[jax.ShapeDtypeStruct((ROUNDS, 2, NB, channels, channels), jnp.bfloat16), token_shape()],
        input_output_aliases=aliases,
        name="cross",
        compiler_params=pltpu.CompilerParams(vmem_limit_bytes=VMEM),
        cost_estimate=SHORT,
    )(*args)


def body(record, owner_order):
    groups, members = lax.axis_size("blk"), lax.axis_size("grp")
    chips = members // CORES
    core_arg = (lax.axis_index("grp") % CORES).reshape(1).astype(jnp.int32)

    flow = [(m, m + CORES) for m in range(0, members - CORES, CORES)]
    flow += [(m + CORES, m) for m in range(1, members - CORES, CORES)]
    swap = [(m, m ^ 1) for m in range(members)]
    chunks = ROUNDS * HALF
    steps = chunks + LAG * (chips - 2)

    mine_a, inv, token = band(core_arg, record, 0, FIRST)
    mine, twin = [mine_a], [lax.ppermute(mine_a[i], "grp", swap) for i in range(FIRST)]

    arrived, held, turned = [], [], []
    out = None
    kept, nears, fars = {}, {}, {}
    todo = {}
    for g in range(chunks // GROUP):
        at = (g + 1) * GROUP - 1 + LAG * (chips - 2) + LAG
        across = bool(ORDER[g][0])
        left = chunks // GROUP - 1 - g
        pick = at + (1, 3, 3)[left] if left < 3 else at + GAP
        give = pick + 5 if across else pick
        meet = (pick + 1, pick + 3, give + 1)[left] if left < 3 else give + GAP
        plan = ((at, "collect", 0), (pick, "select", 0), (give, "pass_over", 0), (meet, "cross", 0), (meet + (left >= 3), "cross", 1))
        for wait, what, part in plan:
            todo.setdefault(wait, []).append((what, g, part))

    for step in range(max(todo) + 1):
        if step < steps + LAG:
            buffer = arrived[step - LAG] if step >= LAG else None
            sent, token = inject(owner_order, token, step, mine, twin, buffer)
            if step < steps:
                arrived.append(lax.ppermute(sent, "grp", flow))
            if step >= LAG:
                held.append(sent)
        if step == REST_AT:
            mine_b, token = band(core_arg, record, FIRST, HALF, inv, token)
            mine.append(mine_b)
            twin += [lax.ppermute(mine_b[i], "grp", swap) for i in range(HALF - FIRST)]
        if step in (5, 7):
            part, token = turn(mine[0] if step == 5 else mine[1], token)
            turned.append(part)
        for what, g, part in todo.get(step, ()):
            first = g * GROUP
            ks = range(first, first + GROUP)
            r, begin = chunk_of(first)
            if what == "collect":
                given, token = gather(owner_order, token, ks, held)
                kept[g] = lax.ppermute(given, "grp", swap)
            elif what == "select":
                near, token = gather(owner_order, token, ks, held, kept[g])
                if r:
                    near = lax.ppermute(near, "blk", [(b, (b + r) % groups) for b in range(groups)])
                nears[g] = near
            elif what == "pass_over":
                fars[g] = lax.ppermute(nears[g], "grp", swap)
            else:
                own, count = turned[begin // FIRST], GROUP // 2
                out, token = cross(out, token, core_arg, own, nears[g], fars[g], r, begin, part * count, count)
    return out


def solution(mesh):
    return jax.shard_map(
        body,
        mesh=mesh,
        in_specs=(P(None, ("blk", "grp")), P()),
        out_specs=P(None, None, None, ("blk", "grp"), None),
        check_vma=False,
    )
```

time: 719 us -> 293 us (0.41)
  waiting for transfers between devices: 590 us -> 42.2 us
  starting transfers between devices: 3.73 us -> 153 us
  Pallas kernels: 0 us -> 90.5 us
  matrix products: 42.6 us -> 0 us
  other arithmetic: 37.4 us -> 0.01 us
  local copies, waits for them, and re-layouts: 28.4 us -> 4.85 us
  between operations: 16.1 us -> 1.15 us
    psum x1 -> x0, waiting for transfers between devices: 321 us -> none  [broadcast(): return lax.psum(kept, axis)]
    ppermute x3 -> x66, waiting for transfers between devices: 269 us -> 42.2 us  [the longest x6 25.7 us: body(): lax.ppermute(near, 'blk', [(b, (b + r) % groups) for b in range(groups)])]
    ppermute x3 -> x66, starting transfers between devices: 3.73 us -> 153 us  [the longest x36 138 us: body(): arrived.append(lax.ppermute(sent, 'grp', flow))]
    pallas_call x0 -> x74, Pallas kernels: none -> 90.5 us  [the longest x16 38.4 us: cross(): pl.pallas_call(cross_kernel, grid_spec=pltpu.PrefetchScalarGridSpec(num_s...]
    dot_general x18 -> x0, matrix products: 42.6 us -> none  [the longest x4 10.3 us: cross_stack(): jnp.einsum('wfi,wfj->fij', real_own, imag_other, preferred_element_type=j...]
    slice x7 -> x0, local copies, waits for them, and re-layouts: 17.8 us -> none  [the longest x3 11.9 us: cross_stack(): real_own, imag_own = (own[:, :NB], own[:, NB:])]
    select_n x4 -> x0, other arithmetic: 17.6 us -> none  [broadcast(): jnp.where(lax.axis_index(axis) == source, value, 0).astype(value.dtype)]
    another operation x6 -> x0, other arithmetic: 12.8 us -> none  [the longest x1 7.01 us: body(): return jnp.stack(results, axis=0).astype(jnp.bfloat16)]
  transfers between devices with their start and end apart: 4 -> 66, of which waited for: 4 -> 21; matrix products, arithmetic and copies ran while one was open for 2% -> 0% of each run, Pallas kernels for 0% -> 27%
where the time goes in v2:
time: 293 us; the launch traced here: 292 us
  starting transfers between devices  153 us (52%)
  Pallas kernels  90.5 us (31%)
  waiting for transfers between devices  42.2 us (14%)
  local copies, waits for them, and re-layouts  4.85 us (2%)
    ppermute x36, starting transfers between devices, body(): arrived.append(lax.ppermute(sent, 'grp', flow))  138 us
    pallas_call x16, Pallas kernels, cross(): pl.pallas_call(cross_kernel, grid_spec=pltpu.PrefetchScalarGridSpec(num_s...  38.4 us
    pallas_call x38, Pallas kernels, inject(): pl.pallas_call(kernel, in_specs=in_specs, out_specs=[in_place()] * 2, out...  27 us
    ppermute x6, waiting for transfers between devices, body(): lax.ppermute(near, 'blk', [(b, (b + r) % groups) for b in range(groups)])  25.7 us
    ppermute x36, waiting for transfers between devices, body(): arrived.append(lax.ppermute(sent, 'grp', flow))  15.4 us
    pallas_call x16, Pallas kernels, gather(): pl.pallas_call(kernel, in_specs=[pl.BlockSpec(memory_space=pltpu.SMEM)] +...  12 us
    pallas_call x2, Pallas kernels, band(): pl.pallas_call(functools.partial(band_kernel, first), grid=(WIN // WG,),...  11.1 us
    ppermute x6, starting transfers between devices, body(): lax.ppermute(near, 'blk', [(b, (b + r) % groups) for b in range(groups)])  10.8 us
  transfers between devices with their start and end apart: 66, of which 21 were waited for; matrix products, arithmetic and copies ran while one was open for 0% of the time, Pallas kernels for 27%

profile of v2, /device:TPU:0, one launch (start us, length us, event | category | flops | bytes accessed | tf_op | source)
XLA Modules:
  0.0 292.0 jit_solution(7101666863163186101)
XLA Ops:
  0.0 3.4 %copy-done = bf16[16448,256]{1,0:T(8,128)(2,1)S(1)} copy-done((bf16[16448,256]{1,0:T(8,128)(2,1)S(1)}, bf16[16448,256]{1,0:T(8,128)(2,1)}, u32[]{:S(2)}) %copy-start) | copy-done | bytes 8421400
  4.5 5.7 %band_first.1 = (bf16[4,2,2,256,256]{4,3,2,1,0:T(8,128)(2,1)S(1)}, f32[256,256]{1,0:T(8,128)S(1)}, s32[8,128]{1,0:T(8,128)S(1)}) custom-call(s32[1]{0:T(128)} %bitcast.core_ref, bf16[16448,256]{1,0:T(8,128)(2,1)S(1)} %copy-done, bf16[16448,256]{1,0:T(8,128)(2,1)S(1)} %copy-done, bf16[256,1088]{1,0:T(8,128)(2,1)S(1)} %copy-done.3), custom_call_target="tpu_custom_call" | custom-call | flops 2281701376 | bytes 12632064 | tf_op jit(solution)/shard_map/band_first/pallas_call | solution.py:106
  13.1 4.8 %collective-permute-start.4 = (bf16[2,2,256,256]{3,2,1,0:T(8,128)(2,1)S(1)}, bf16[2,2,256,256]{3,2,1,0:T(8,128)(2,1)S(1)}, u32[]{:S(2)}, u32[]{:S(2)}) collective-permute-start(bf16[2,2,256,256]{3,2,1,0:T(8,128)(2,1)S(1)} %get-tuple-element.160), channel_id=1, source_target_pairs={{0,2},{2,4},{4,6},{3,1},{5,3},{7,5},{8,10},{10,12},{12,14},{11,9},... | collective-permute-start | bytes 1572872 | tf_op jit(solution)/shard_map/ppermute | solution.py:344
  18.7 3.4 %collective-permute-start.5 = (bf16[2,2,256,256]{3,2,1,0:T(8,128)(2,1)S(1)}, bf16[2,2,256,256]{3,2,1,0:T(8,128)(2,1)S(1)}, u32[]{:S(2)}, u32[]{:S(2)}) collective-permute-start(bf16[2,2,256,256]{3,2,1,0:T(8,128)(2,1)S(1)} %get-tuple-element.162), channel_id=1, source_target_pairs={{0,2},{2,4},{4,6},{3,1},{5,3},{7,5},{8,10},{10,12},{12,14},{11,9},... | collective-permute-start | bytes 1572872 | tf_op jit(solution)/shard_map/ppermute | solution.py:344
  22.2 5.4 %band_rest.1 = (bf16[4,2,2,256,256]{4,3,2,1,0:T(8,128)(2,1)S(1)}, s32[8,128]{1,0:T(8,128)S(1)}) custom-call(s32[1]{0:T(128)} %bitcast.core_ref, bf16[16448,256]{1,0:T(8,128)(2,1)S(1)} %bitcast.18, bf16[16448,256]{1,0:T(8,128)(2,1)S(1)} %bitcast.18, bf16[256,1088]{1,0:T(8,128)(2,1)S(1)} %copy-done.2, f32[256,256]{1,0:T(8,128)S(1)} %get-tuple-element.153.refs_0_, ...), custom_call_target="tpu_custom_call" | custom-call | flops 2281701376 | bytes 12632064 | tf_op jit(solution)/shard_map/band_rest/pallas_call | solution.py:106
  28.3 3.3 %collective-permute-start.6 = (bf16[2,2,256,256]{3,2,1,0:T(8,128)(2,1)S(1)}, bf16[2,2,256,256]{3,2,1,0:T(8,128)(2,1)S(1)}, u32[]{:S(2)}, u32[]{:S(2)}) collective-permute-start(bf16[2,2,256,256]{3,2,1,0:T(8,128)(2,1)S(1)} %get-tuple-element.164.refs_0_), channel_id=1, source_target_pairs={{0,2},{2,4},{4,6},{3,1},{5,3},{7,5},{8,10},{10,12},{12,14},{11,9},... | collective-permute-start | bytes 1572872 | tf_op jit(solution)/shard_map/ppermute | solution.py:344
  32.4 2.9 collective-permute-start.7
  35.3 3.0 %collective-permute-done.6.refs_4_ = bf16[2,2,256,256]{3,2,1,0:T(8,128)(2,1)S(1)} collective-permute-done((bf16[2,2,256,256]{3,2,1,0:T(8,128)(2,1)S(1)}, bf16[2,2,256,256]{3,2,1,0:T(8,128)(2,1)S(1)}, u32[]{:S(2)}, u32[]{:S(2)}) %collective-permute-start.6) | collective-permute-done | bytes 524320 | tf_op jit(solution)/shard_map/ppermute | solution.py:344
  39.0 4.4 %collective-permute-start.8 = (bf16[2,2,256,256]{3,2,1,0:T(8,128)(2,1)S(1)}, bf16[2,2,256,256]{3,2,1,0:T(8,128)(2,1)S(1)}, u32[]{:S(2)}, u32[]{:S(2)}) collective-permute-start(bf16[2,2,256,256]{3,2,1,0:T(8,128)(2,1)S(1)} %get-tuple-element.169.refs_1_), channel_id=1, source_target_pairs={{0,2},{2,4},{4,6},{3,1},{5,3},{7,5},{8,10},{10,12},{12,14},{11,9},... | collective-permute-start | bytes 1572872 | tf_op jit(solution)/shard_map/ppermute | solution.py:344
  44.6 4.4 %collective-permute-start.9 = (bf16[2,2,256,256]{3,2,1,0:T(8,128)(2,1)S(1)}, bf16[2,2,256,256]{3,2,1,0:T(8,128)(2,1)S(1)}, u32[]{:S(2)}, u32[]{:S(2)}) collective-permute-start(bf16[2,2,256,256]{3,2,1,0:T(8,128)(2,1)S(1)} %get-tuple-element.171.refs_4_), channel_id=1, source_target_pairs={{0,2},{2,4},{4,6},{3,1},{5,3},{7,5},{8,10},{10,12},{12,14},{11,9},... | collective-permute-start | bytes 1572872 | tf_op jit(solution)/shard_map/ppermute | solution.py:344
  50.8 4.4 %collective-permute-start.12 = (bf16[2,2,256,256]{3,2,1,0:T(8,128)(2,1)S(1)}, bf16[2,2,256,256]{3,2,1,0:T(8,128)(2,1)S(1)}, u32[]{:S(2)}, u32[]{:S(2)}) collective-permute-start(bf16[2,2,256,256]{3,2,1,0:T(8,128)(2,1)S(1)} %get-tuple-element.174.refs_2_.refs_0_), channel_id=1, source_target_pairs={{0,2},{2,4},{4,6},{3,1},{5,3},{7,5},{8,10},{10,12},{12,14},{11,9},... | collective-permute-start | bytes 1572872 | tf_op jit(solution)/shard_map/ppermute | solution.py:344
  56.4 4.4 %collective-permute-start.13 = (bf16[2,2,256,256]{3,2,1,0:T(8,128)(2,1)S(1)}, bf16[2,2,256,256]{3,2,1,0:T(8,128)(2,1)S(1)}, u32[]{:S(2)}, u32[]{:S(2)}) collective-permute-start(bf16[2,2,256,256]{3,2,1,0:T(8,128)(2,1)S(1)} %get-tuple-element.175.refs_5_.refs_3_), channel_id=1, source_target_pairs={{0,2},{2,4},{4,6},{3,1},{5,3},{7,5},{8,10},{10,12},{12,14},{11,9},... | collective-permute-start | bytes 1572872 | tf_op jit(solution)/shard_map/ppermute | solution.py:344
  62.6 4.4 %collective-permute-start.14 = (bf16[2,2,256,256]{3,2,1,0:T(8,128)(2,1)S(1)}, bf16[2,2,256,256]{3,2,1,0:T(8,128)(2,1)S(1)}, u32[]{:S(2)}, u32[]{:S(2)}) collective-permute-start(bf16[2,2,256,256]{3,2,1,0:T(8,128)(2,1)S(1)} %get-tuple-element.177.refs_6_.refs_1_), channel_id=1, source_target_pairs={{0,2},{2,4},{4,6},{3,1},{5,3},{7,5},{8,10},{10,12},{12,14},{11,9},... | collective-permute-start | bytes 1572872 | tf_op jit(solution)/shard_map/ppermute | solution.py:344
  68.1 4.4 %collective-permute-start.15 = (bf16[2,2,256,256]{3,2,1,0:T(8,128)(2,1)S(1)}, bf16[2,2,256,256]{3,2,1,0:T(8,128)(2,1)S(1)}, u32[]{:S(2)}, u32[]{:S(2)}) collective-permute-start(bf16[2,2,256,256]{3,2,1,0:T(8,128)(2,1)S(1)} %get-tuple-element.179.refs_7_.refs_4_), channel_id=1, source_target_pairs={{0,2},{2,4},{4,6},{3,1},{5,3},{7,5},{8,10},{10,12},{12,14},{11,9},... | collective-permute-start | bytes 1572872 | tf_op jit(solution)/shard_map/ppermute | solution.py:344
  74.3 4.5 %collective-permute-start.16 = (bf16[2,2,256,256]{3,2,1,0:T(8,128)(2,1)S(1)}, bf16[2,2,256,256]{3,2,1,0:T(8,128)(2,1)S(1)}, u32[]{:S(2)}, u32[]{:S(2)}) collective-permute-start(bf16[2,2,256,256]{3,2,1,0:T(8,128)(2,1)S(1)} %get-tuple-element.182.refs_2_.refs_0_), channel_id=1, source_target_pairs={{0,2},{2,4},{4,6},{3,1},{5,3},{7,5},{8,10},{10,12},{12,14},{11,9},... | collective-permute-start | bytes 1572872 | tf_op jit(solution)/shard_map/ppermute | solution.py:344
  79.9 4.5 %collective-permute-start.18 = (bf16[2,2,256,256]{3,2,1,0:T(8,128)(2,1)S(1)}, bf16[2,2,256,256]{3,2,1,0:T(8,128)(2,1)S(1)}, u32[]{:S(2)}, u32[]{:S(2)}) collective-permute-start(bf16[2,2,256,256]{3,2,1,0:T(8,128)(2,1)S(1)} %get-tuple-element.186.refs_5_.refs_3_), channel_id=1, source_target_pairs={{0,2},{2,4},{4,6},{3,1},{5,3},{7,5},{8,10},{10,12},{12,14},{11,9},... | collective-permute-start | bytes 1572872 | tf_op jit(solution)/shard_map/ppermute | solution.py:344
  86.2 4.4 %collective-permute-start.19 = (bf16[2,2,256,256]{3,2,1,0:T(8,128)(2,1)S(1)}, bf16[2,2,256,256]{3,2,1,0:T(8,128)(2,1)S(1)}, u32[]{:S(2)}, u32[]{:S(2)}) collective-permute-start(bf16[2,2,256,256]{3,2,1,0:T(8,128)(2,1)S(1)} %get-tuple-element.185.refs_6_.refs_1_), channel_id=1, source_target_pairs={{0,2},{2,4},{4,6},{3,1},{5,3},{7,5},{8,10},{10,12},{12,14},{11,9},... | collective-permute-start | bytes 1572872 | tf_op jit(solution)/shard_map/ppermute | solution.py:344
  91.8 4.4 %collective-permute-start.22 = (bf16[2,2,256,256]{3,2,1,0:T(8,128)(2,1)S(1)}, bf16[2,2,256,256]{3,2,1,0:T(8,128)(2,1)S(1)}, u32[]{:S(2)}, u32[]{:S(2)}) collective-permute-start(bf16[2,2,256,256]{3,2,1,0:T(8,128)(2,1)S(1)} %get-tuple-element.188.refs_7_.refs_4_), channel_id=1, source_target_pairs={{0,2},{2,4},{4,6},{3,1},{5,3},{7,5},{8,10},{10,12},{12,14},{11,9},... | collective-permute-start | bytes 1572872 | tf_op jit(solution)/shard_map/ppermute | solution.py:344
  98.1 4.3 %collective-permute-start.23 = (bf16[2,2,256,256]{3,2,1,0:T(8,128)(2,1)S(1)}, bf16[2,2,256,256]{3,2,1,0:T(8,128)(2,1)S(1)}, u32[]{:S(2)}, u32[]{:S(2)}) collective-permute-start(bf16[2,2,256,256]{3,2,1,0:T(8,128)(2,1)S(1)} %get-tuple-element.191.refs_2_.refs_0_), channel_id=1, source_target_pairs={{0,2},{2,4},{4,6},{3,1},{5,3},{7,5},{8,10},{10,12},{12,14},{11,9},... | collective-permute-start | bytes 1572872 | tf_op jit(solution)/shard_map/ppermute | solution.py:344
  104.0 4.1 %collective-permute-start.24 = (bf16[2,2,256,256]{3,2,1,0:T(8,128)(2,1)S(1)}, bf16[2,2,256,256]{3,2,1,0:T(8,128)(2,1)S(1)}, u32[]{:S(2)}, u32[]{:S(2)}) collective-permute-start(bf16[2,2,256,256]{3,2,1,0:T(8,128)(2,1)S(1)} %get-tuple-element.195.refs_5_.refs_3_), channel_id=1, source_target_pairs={{0,2},{2,4},{4,6},{3,1},{5,3},{7,5},{8,10},{10,12},{12,14},{11,9},... | collective-permute-start | bytes 1572872 | tf_op jit(solution)/shard_map/ppermute | solution.py:344
  109.8 4.4 %collective-permute-start.25 = (bf16[2,2,256,256]{3,2,1,0:T(8,128)(2,1)S(1)}, bf16[2,2,256,256]{3,2,1,0:T(8,128)(2,1)S(1)}, u32[]{:S(2)}, u32[]{:S(2)}) collective-permute-start(bf16[2,2,256,256]{3,2,1,0:T(8,128)(2,1)S(1)} %get-tuple-element.197.refs_6_.refs_1_), channel_id=1, source_target_pairs={{0,2},{2,4},{4,6},{3,1},{5,3},{7,5},{8,10},{10,12},{12,14},{11,9},... | collective-permute-start | bytes 1572872 | tf_op jit(solution)/shard_map/ppermute | solution.py:344
  115.4 4.4 %collective-permute-start.27 = (bf16[2,2,256,256]{3,2,1,0:T(8,128)(2,1)S(1)}, bf16[2,2,256,256]{3,2,1,0:T(8,128)(2,1)S(1)}, u32[]{:S(2)}, u32[]{:S(2)}) collective-permute-start(bf16[2,2,256,256]{3,2,1,0:T(8,128)(2,1)S(1)} %get-tuple-element.199.refs_7_.refs_4_), channel_id=1, source_target_pairs={{0,2},{2,4},{4,6},{3,1},{5,3},{7,5},{8,10},{10,12},{12,14},{11,9},... | collective-permute-start | bytes 1572872 | tf_op jit(solution)/shard_map/ppermute | solution.py:344
  123.1 2.9 collective-permute-start.28
  127.5 4.1 %collective-permute-start.29 = (bf16[2,2,256,256]{3,2,1,0:T(8,128)(2,1)S(1)}, bf16[2,2,256,256]{3,2,1,0:T(8,128)(2,1)S(1)}, u32[]{:S(2)}, u32[]{:S(2)}) collective-permute-start(bf16[2,2,256,256]{3,2,1,0:T(8,128)(2,1)S(1)} %get-tuple-element.208.refs_5_.refs_3_), channel_id=1, source_target_pairs={{0,2},{2,4},{4,6},{3,1},{5,3},{7,5},{8,10},{10,12},{12,14},{11,9},... | collective-permute-start | bytes 1572872 | tf_op jit(solution)/shard_map/ppermute | solution.py:344
  133.3 4.4 %collective-permute-start.30 = (bf16[2,2,256,256]{3,2,1,0:T(8,128)(2,1)S(1)}, bf16[2,2,256,256]{3,2,1,0:T(8,128)(2,1)S(1)}, u32[]{:S(2)}, u32[]{:S(2)}) collective-permute-start(bf16[2,2,256,256]{3,2,1,0:T(8,128)(2,1)S(1)} %get-tuple-element.207.refs_6_.refs_1_), channel_id=1, source_target_pairs={{0,2},{2,4},{4,6},{3,1},{5,3},{7,5},{8,10},{10,12},{12,14},{11,9},... | collective-permute-start | bytes 1572872 | tf_op jit(solution)/shard_map/ppermute | solution.py:344
  142.0 4.3 %collective-permute-start.32 = (bf16[2,2,256,256]{3,2,1,0:T(8,128)(2,1)S(1)}, bf16[2,2,256,256]{3,2,1,0:T(8,128)(2,1)S(1)}, u32[]{:S(2)}, u32[]{:S(2)}) collective-permute-start(bf16[2,2,256,256]{3,2,1,0:T(8,128)(2,1)S(1)} %get-tuple-element.210.refs_7_.refs_4_), channel_id=1, source_target_pairs={{0,2},{2,4},{4,6},{3,1},{5,3},{7,5},{8,10},{10,12},{12,14},{11,9},... | collective-permute-start | bytes 1572872 | tf_op jit(solution)/shard_map/ppermute | solution.py:344
  147.8 2.5 collective-permute-start.33
  153.7 4.5 %collective-permute-start.36 = (bf16[2,2,256,256]{3,2,1,0:T(8,128)(2,1)S(1)}, bf16[2,2,256,256]{3,2,1,0:T(8,128)(2,1)S(1)}, u32[]{:S(2)}, u32[]{:S(2)}) collective-permute-start(bf16[2,2,256,256]{3,2,1,0:T(8,128)(2,1)S(1)} %get-tuple-element.217.refs_5_.refs_3_), channel_id=1, source_target_pairs={{0,2},{2,4},{4,6},{3,1},{5,3},{7,5},{8,10},{10,12},{12,14},{11,9},... | collective-permute-start | bytes 1572872 | tf_op jit(solution)/shard_map/ppermute | solution.py:344
  159.4 4.4 %collective-permute-start.38 = (bf16[2,2,256,256]{3,2,1,0:T(8,128)(2,1)S(1)}, bf16[2,2,256,256]{3,2,1,0:T(8,128)(2,1)S(1)}, u32[]{:S(2)}, u32[]{:S(2)}) collective-permute-start(bf16[2,2,256,256]{3,2,1,0:T(8,128)(2,1)S(1)} %get-tuple-element.219.refs_6_.refs_1_), channel_id=1, source_target_pairs={{0,2},{2,4},{4,6},{3,1},{5,3},{7,5},{8,10},{10,12},{12,14},{11,9},... | collective-permute-start | bytes 1572872 | tf_op jit(solution)/shard_map/ppermute | solution.py:344
  168.8 2.5 collective-permute-start.40
  171.2 2.4 cross.17
  179.2 3.8 %collective-permute-start.44 = (bf16[2,2,256,256]{3,2,1,0:T(8,128)(2,1)S(1)}, bf16[2,2,256,256]{3,2,1,0:T(8,128)(2,1)S(1)}, u32[]{:S(2)}, u32[]{:S(2)}) collective-permute-start(bf16[2,2,256,256]{3,2,1,0:T(8,128)(2,1)S(1)} %get-tuple-element.234.refs_5_.refs_3_), channel_id=1, source_target_pairs={{0,2},{2,4},{4,6},{3,1},{5,3},{7,5},{8,10},{10,12},{12,14},{11,9},... | collective-permute-start | bytes 1572872 | tf_op jit(solution)/shard_map/ppermute | solution.py:344
  185.0 4.3 %collective-permute-start.45 = (bf16[2,2,256,256]{3,2,1,0:T(8,128)(2,1)S(1)}, bf16[2,2,256,256]{3,2,1,0:T(8,128)(2,1)S(1)}, u32[]{:S(2)}, u32[]{:S(2)}) collective-permute-start(bf16[2,2,256,256]{3,2,1,0:T(8,128)(2,1)S(1)} %get-tuple-element.236.refs_6_.refs_1_), channel_id=1, source_target_pairs={{0,2},{2,4},{4,6},{3,1},{5,3},{7,5},{8,10},{10,12},{12,14},{11,9},... | collective-permute-start | bytes 1572872 | tf_op jit(solution)/shard_map/ppermute | solution.py:344
  194.5 2.4 cross.19
  198.1 2.7 collective-permute-start.48
  204.7 2.7 collective-permute-done.48.refs_7_
  208.2 4.3 %collective-permute-start.53 = (bf16[2,2,256,256]{3,2,1,0:T(8,128)(2,1)S(1)}, bf16[2,2,256,256]{3,2,1,0:T(8,128)(2,1)S(1)}, u32[]{:S(2)}, u32[]{:S(2)}) collective-permute-start(bf16[2,2,256,256]{3,2,1,0:T(8,128)(2,1)S(1)} %get-tuple-element.252.refs_5_.refs_3_), channel_id=1, source_target_pairs={{0,2},{2,4},{4,6},{3,1},{5,3},{7,5},{8,10},{10,12},{12,14},{11,9},... | collective-permute-start | bytes 1572872 | tf_op jit(solution)/shard_map/ppermute | solution.py:344
  214.0 4.3 %collective-permute-start.54 = (bf16[2,2,256,256]{3,2,1,0:T(8,128)(2,1)S(1)}, bf16[2,2,256,256]{3,2,1,0:T(8,128)(2,1)S(1)}, u32[]{:S(2)}, u32[]{:S(2)}) collective-permute-start(bf16[2,2,256,256]{3,2,1,0:T(8,128)(2,1)S(1)} %get-tuple-element.251.refs_6_.refs_1_), channel_id=1, source_target_pairs={{0,2},{2,4},{4,6},{3,1},{5,3},{7,5},{8,10},{10,12},{12,14},{11,9},... | collective-permute-start | bytes 1572872 | tf_op jit(solution)/shard_map/ppermute | solution.py:344
  218.3 2.4 cross.20
  221.5 2.5 collective-permute-start.62
  224.7 2.6 collective-permute-start.55
  227.3 2.4 cross.21
  234.6 4.4 %collective-permute-start.60 = (bf16[2,2,256,256]{3,2,1,0:T(8,128)(2,1)S(1)}, bf16[2,2,256,256]{3,2,1,0:T(8,128)(2,1)S(1)}, u32[]{:S(2)}, u32[]{:S(2)}) collective-permute-start(bf16[2,2,256,256]{3,2,1,0:T(8,128)(2,1)S(1)} %get-tuple-element.266.refs_5_), channel_id=1, source_target_pairs={{0,2},{2,4},{4,6},{3,1},{5,3},{7,5},{8,10},{10,12},{12,14},{11,9},... | collective-permute-start | bytes 1572872 | tf_op jit(solution)/shard_map/ppermute | solution.py:344
  239.0 5.2 %collective-permute-done.62.near_ref = bf16[4,2,256,256]{3,2,1,0:T(8,128)(2,1)S(1)} collective-permute-done((bf16[4,2,256,256]{3,2,1,0:T(8,128)(2,1)S(1)}, bf16[4,2,256,256]{3,2,1,0:T(8,128)(2,1)S(1)}, u32[]{:S(2)}, u32[]{:S(2)}) %collective-permute-start.62) | collective-permute-done | bytes 1048608 | tf_op jit(solution)/shard_map/ppermute | solution.py:364
  244.8 2.4 cross.22
  248.6 2.4 cross.23
  259.9 17.8 %collective-permute-done.46.near_ref = bf16[4,2,256,256]{3,2,1,0:T(8,128)(2,1)S(1)} collective-permute-done((bf16[4,2,256,256]{3,2,1,0:T(8,128)(2,1)S(1)}, bf16[4,2,256,256]{3,2,1,0:T(8,128)(2,1)S(1)}, u32[]{:S(2)}, u32[]{:S(2)}) %collective-permute-start.46) | collective-permute-done | bytes 1048608 | tf_op jit(solution)/shard_map/ppermute | solution.py:364
  277.7 2.4 cross.26
  (175 shorter events, 96.2 us)
Async XLA Ops:
  10.9 16.7 %collective-permute-start.3 = (bf16[2,2,256,256]{3,2,1,0:T(8,128)(2,1)S(1)}, bf16[2,2,256,256]{3,2,1,0:T(8,128)(2,1)S(1)}, u32[]{:S(2)}, u32[]{:S(2)}) collective-permute-start(bf16[2,2,256,256]{3,2,1,0:T(8,128)(2,1)S(1)} %get-tuple-element.305), channel_id=1, source_target_pairs={{0,1},{1,0},{2,3},{3,2},{4,5},{5,4},{6,7},{7,6},{8,9},{9,8},{10,11... | collective-permute-start | bytes 1572872 | tf_op jit(solution)/shard_map/ppermute | solution.py:322
  13.1 14.5 %collective-permute-start.4 = (bf16[2,2,256,256]{3,2,1,0:T(8,128)(2,1)S(1)}, bf16[2,2,256,256]{3,2,1,0:T(8,128)(2,1)S(1)}, u32[]{:S(2)}, u32[]{:S(2)}) collective-permute-start(bf16[2,2,256,256]{3,2,1,0:T(8,128)(2,1)S(1)} %get-tuple-element.160), channel_id=1, source_target_pairs={{0,2},{2,4},{4,6},{3,1},{5,3},{7,5},{8,10},{10,12},{12,14},{11,9},... | collective-permute-start | bytes 1572872 | tf_op jit(solution)/shard_map/ppermute | solution.py:344
  17.9 13.7 %collective-permute-start.2 = (bf16[2,2,256,256]{3,2,1,0:T(8,128)(2,1)S(1)}, bf16[2,2,256,256]{3,2,1,0:T(8,128)(2,1)S(1)}, u32[]{:S(2)}, u32[]{:S(2)}) collective-permute-start(bf16[2,2,256,256]{3,2,1,0:T(8,128)(2,1)S(1)} %get-tuple-element.306), channel_id=1, source_target_pairs={{0,1},{1,0},{2,3},{3,2},{4,5},{5,4},{6,7},{7,6},{8,9},{9,8},{10,11... | collective-permute-start | bytes 1572872 | tf_op jit(solution)/shard_map/ppermute | solution.py:322
  18.7 12.9 %collective-permute-start.5 = (bf16[2,2,256,256]{3,2,1,0:T(8,128)(2,1)S(1)}, bf16[2,2,256,256]{3,2,1,0:T(8,128)(2,1)S(1)}, u32[]{:S(2)}, u32[]{:S(2)}) collective-permute-start(bf16[2,2,256,256]{3,2,1,0:T(8,128)(2,1)S(1)} %get-tuple-element.162), channel_id=1, source_target_pairs={{0,2},{2,4},{4,6},{3,1},{5,3},{7,5},{8,10},{10,12},{12,14},{11,9},... | collective-permute-start | bytes 1572872 | tf_op jit(solution)/shard_map/ppermute | solution.py:344
  32.4 11.5 %collective-permute-start.7 = (bf16[2,2,256,256]{3,2,1,0:T(8,128)(2,1)S(1)}, bf16[2,2,256,256]{3,2,1,0:T(8,128)(2,1)S(1)}, u32[]{:S(2)}, u32[]{:S(2)}) collective-permute-start(bf16[2,2,256,256]{3,2,1,0:T(8,128)(2,1)S(1)} %get-tuple-element.166.refs_3_), channel_id=1, source_target_pairs={{0,2},{2,4},{4,6},{3,1},{5,3},{7,5},{8,10},{10,12},{12,14},{11,9},... | collective-permute-start | bytes 1572872 | tf_op jit(solution)/shard_map/ppermute | solution.py:344
  39.0 11.1 %collective-permute-start.8 = (bf16[2,2,256,256]{3,2,1,0:T(8,128)(2,1)S(1)}, bf16[2,2,256,256]{3,2,1,0:T(8,128)(2,1)S(1)}, u32[]{:S(2)}, u32[]{:S(2)}) collective-permute-start(bf16[2,2,256,256]{3,2,1,0:T(8,128)(2,1)S(1)} %get-tuple-element.169.refs_1_), channel_id=1, source_target_pairs={{0,2},{2,4},{4,6},{3,1},{5,3},{7,5},{8,10},{10,12},{12,14},{11,9},... | collective-permute-start | bytes 1572872 | tf_op jit(solution)/shard_map/ppermute | solution.py:344
  44.6 11.1 %collective-permute-start.9 = (bf16[2,2,256,256]{3,2,1,0:T(8,128)(2,1)S(1)}, bf16[2,2,256,256]{3,2,1,0:T(8,128)(2,1)S(1)}, u32[]{:S(2)}, u32[]{:S(2)}) collective-permute-start(bf16[2,2,256,256]{3,2,1,0:T(8,128)(2,1)S(1)} %get-tuple-element.171.refs_4_), channel_id=1, source_target_pairs={{0,2},{2,4},{4,6},{3,1},{5,3},{7,5},{8,10},{10,12},{12,14},{11,9},... | collective-permute-start | bytes 1572872 | tf_op jit(solution)/shard_map/ppermute | solution.py:344
  56.4 11.1 %collective-permute-start.13 = (bf16[2,2,256,256]{3,2,1,0:T(8,128)(2,1)S(1)}, bf16[2,2,256,256]{3,2,1,0:T(8,128)(2,1)S(1)}, u32[]{:S(2)}, u32[]{:S(2)}) collective-permute-start(bf16[2,2,256,256]{3,2,1,0:T(8,128)(2,1)S(1)} %get-tuple-element.175.refs_5_.refs_3_), channel_id=1, source_target_pairs={{0,2},{2,4},{4,6},{3,1},{5,3},{7,5},{8,10},{10,12},{12,14},{11,9},... | collective-permute-start | bytes 1572872 | tf_op jit(solution)/shard_map/ppermute | solution.py:344
  72.8 11.7 %collective-permute-start.11 = (bf16[2,2,256,256]{3,2,1,0:T(8,128)(2,1)S(1)}, bf16[2,2,256,256]{3,2,1,0:T(8,128)(2,1)S(1)}, u32[]{:S(2)}, u32[]{:S(2)}) collective-permute-start(bf16[2,2,256,256]{3,2,1,0:T(8,128)(2,1)S(1)} %get-tuple-element.303), channel_id=1, source_target_pairs={{0,1},{1,0},{2,3},{3,2},{4,5},{5,4},{6,7},{7,6},{8,9},{9,8},{10,11... | collective-permute-start | bytes 1572872 | tf_op jit(solution)/shard_map/ppermute | solution.py:350
  74.3 11.1 %collective-permute-start.16 = (bf16[2,2,256,256]{3,2,1,0:T(8,128)(2,1)S(1)}, bf16[2,2,256,256]{3,2,1,0:T(8,128)(2,1)S(1)}, u32[]{:S(2)}, u32[]{:S(2)}) collective-permute-start(bf16[2,2,256,256]{3,2,1,0:T(8,128)(2,1)S(1)} %get-tuple-element.182.refs_2_.refs_0_), channel_id=1, source_target_pairs={{0,2},{2,4},{4,6},{3,1},{5,3},{7,5},{8,10},{10,12},{12,14},{11,9},... | collective-permute-start | bytes 1572872 | tf_op jit(solution)/shard_map/ppermute | solution.py:344
  78.8 11.9 %collective-permute-start.17 = (bf16[2,2,256,256]{3,2,1,0:T(8,128)(2,1)S(1)}, bf16[2,2,256,256]{3,2,1,0:T(8,128)(2,1)S(1)}, u32[]{:S(2)}, u32[]{:S(2)}) collective-permute-start(bf16[2,2,256,256]{3,2,1,0:T(8,128)(2,1)S(1)} %get-tuple-element.302), channel_id=1, source_target_pairs={{0,1},{1,0},{2,3},{3,2},{4,5},{5,4},{6,7},{7,6},{8,9},{9,8},{10,11... | collective-permute-start | bytes 1572872 | tf_op jit(solution)/shard_map/ppermute | solution.py:350
  79.9 11.1 %collective-permute-start.18 = (bf16[2,2,256,256]{3,2,1,0:T(8,128)(2,1)S(1)}, bf16[2,2,256,256]{3,2,1,0:T(8,128)(2,1)S(1)}, u32[]{:S(2)}, u32[]{:S(2)}) collective-permute-start(bf16[2,2,256,256]{3,2,1,0:T(8,128)(2,1)S(1)} %get-tuple-element.186.refs_5_.refs_3_), channel_id=1, source_target_pairs={{0,2},{2,4},{4,6},{3,1},{5,3},{7,5},{8,10},{10,12},{12,14},{11,9},... | collective-permute-start | bytes 1572872 | tf_op jit(solution)/shard_map/ppermute | solution.py:344
  84.4 18.0 %collective-permute-start.21 = (bf16[4,2,256,256]{3,2,1,0:T(8,128)(2,1)S(1)}, bf16[4,2,256,256]{3,2,1,0:T(8,128)(2,1)S(1)}, u32[]{:S(2)}, u32[]{:S(2)}) collective-permute-start(bf16[4,2,256,256]{3,2,1,0:T(8,128)(2,1)S(1)} %get-tuple-element.192), channel_id=1, source_target_pairs={{0,1},{1,0},{2,3},{3,2},{4,5},{5,4},{6,7},{7,6},{8,9},{9,8},{10,11... | collective-permute-start | bytes 3145736 | tf_op jit(solution)/shard_map/ppermute | solution.py:360
  84.5 12.5 %collective-permute-start.10 = (bf16[2,2,256,256]{3,2,1,0:T(8,128)(2,1)S(1)}, bf16[2,2,256,256]{3,2,1,0:T(8,128)(2,1)S(1)}, u32[]{:S(2)}, u32[]{:S(2)}) collective-permute-start(bf16[2,2,256,256]{3,2,1,0:T(8,128)(2,1)S(1)} %get-tuple-element.304), channel_id=1, source_target_pairs={{0,1},{1,0},{2,3},{3,2},{4,5},{5,4},{6,7},{7,6},{8,9},{9,8},{10,11... | collective-permute-start | bytes 1572872 | tf_op jit(solution)/shard_map/ppermute | solution.py:350
  86.2 11.1 %collective-permute-start.19 = (bf16[2,2,256,256]{3,2,1,0:T(8,128)(2,1)S(1)}, bf16[2,2,256,256]{3,2,1,0:T(8,128)(2,1)S(1)}, u32[]{:S(2)}, u32[]{:S(2)}) collective-permute-start(bf16[2,2,256,256]{3,2,1,0:T(8,128)(2,1)S(1)} %get-tuple-element.185.refs_6_.refs_1_), channel_id=1, source_target_pairs={{0,2},{2,4},{4,6},{3,1},{5,3},{7,5},{8,10},{10,12},{12,14},{11,9},... | collective-permute-start | bytes 1572872 | tf_op jit(solution)/shard_map/ppermute | solution.py:344
  90.7 12.5 %collective-permute-start.20 = (bf16[2,2,256,256]{3,2,1,0:T(8,128)(2,1)S(1)}, bf16[2,2,256,256]{3,2,1,0:T(8,128)(2,1)S(1)}, u32[]{:S(2)}, u32[]{:S(2)}) collective-permute-start(bf16[2,2,256,256]{3,2,1,0:T(8,128)(2,1)S(1)} %get-tuple-element.301), channel_id=1, source_target_pairs={{0,1},{1,0},{2,3},{3,2},{4,5},{5,4},{6,7},{7,6},{8,9},{9,8},{10,11... | collective-permute-start | bytes 1572872 | tf_op jit(solution)/shard_map/ppermute | solution.py:350
  91.8 11.4 %collective-permute-start.22 = (bf16[2,2,256,256]{3,2,1,0:T(8,128)(2,1)S(1)}, bf16[2,2,256,256]{3,2,1,0:T(8,128)(2,1)S(1)}, u32[]{:S(2)}, u32[]{:S(2)}) collective-permute-start(bf16[2,2,256,256]{3,2,1,0:T(8,128)(2,1)S(1)} %get-tuple-element.188.refs_7_.refs_4_), channel_id=1, source_target_pairs={{0,2},{2,4},{4,6},{3,1},{5,3},{7,5},{8,10},{10,12},{12,14},{11,9},... | collective-permute-start | bytes 1572872 | tf_op jit(solution)/shard_map/ppermute | solution.py:344
  108.0 18.0 %collective-permute-start.26 = (bf16[4,2,256,256]{3,2,1,0:T(8,128)(2,1)S(1)}, bf16[4,2,256,256]{3,2,1,0:T(8,128)(2,1)S(1)}, u32[]{:S(2)}, u32[]{:S(2)}) collective-permute-start(bf16[4,2,256,256]{3,2,1,0:T(8,128)(2,1)S(1)} %get-tuple-element.203), channel_id=1, source_target_pairs={{0,1},{1,0},{2,3},{3,2},{4,5},{5,4},{6,7},{7,6},{8,9},{9,8},{10,11... | collective-permute-start | bytes 3145736 | tf_op jit(solution)/shard_map/ppermute | solution.py:360
  109.8 12.6 %collective-permute-start.25 = (bf16[2,2,256,256]{3,2,1,0:T(8,128)(2,1)S(1)}, bf16[2,2,256,256]{3,2,1,0:T(8,128)(2,1)S(1)}, u32[]{:S(2)}, u32[]{:S(2)}) collective-permute-start(bf16[2,2,256,256]{3,2,1,0:T(8,128)(2,1)S(1)} %get-tuple-element.197.refs_6_.refs_1_), channel_id=1, source_target_pairs={{0,2},{2,4},{4,6},{3,1},{5,3},{7,5},{8,10},{10,12},{12,14},{11,9},... | collective-permute-start | bytes 1572872 | tf_op jit(solution)/shard_map/ppermute | solution.py:344
  115.4 11.4 %collective-permute-start.27 = (bf16[2,2,256,256]{3,2,1,0:T(8,128)(2,1)S(1)}, bf16[2,2,256,256]{3,2,1,0:T(8,128)(2,1)S(1)}, u32[]{:S(2)}, u32[]{:S(2)}) collective-permute-start(bf16[2,2,256,256]{3,2,1,0:T(8,128)(2,1)S(1)} %get-tuple-element.199.refs_7_.refs_4_), channel_id=1, source_target_pairs={{0,2},{2,4},{4,6},{3,1},{5,3},{7,5},{8,10},{10,12},{12,14},{11,9},... | collective-permute-start | bytes 1572872 | tf_op jit(solution)/shard_map/ppermute | solution.py:344
  119.8 21.5 %collective-permute-start.34 = (bf16[4,2,256,256]{3,2,1,0:T(8,128)(2,1)S(1)}, bf16[4,2,256,256]{3,2,1,0:T(8,128)(2,1)S(1)}, u32[]{:S(2)}, u32[]{:S(2)}) collective-permute-start(bf16[4,2,256,256]{3,2,1,0:T(8,128)(2,1)S(1)} %get-tuple-element.221), channel_id=1, source_target_pairs={{0,8},{8,16},{16,24},{24,0},{1,9},{9,17},{17,25},{25,1},{2,10},{10... | collective-permute-start | bytes 3145736 | tf_op jit(solution)/shard_map/ppermute | solution.py:364
  126.0 24.3 %collective-permute-start.31 = (bf16[4,2,256,256]{3,2,1,0:T(8,128)(2,1)S(1)}, bf16[4,2,256,256]{3,2,1,0:T(8,128)(2,1)S(1)}, u32[]{:S(2)}, u32[]{:S(2)}) collective-permute-start(bf16[4,2,256,256]{3,2,1,0:T(8,128)(2,1)S(1)} %get-tuple-element.214), channel_id=1, source_target_pairs={{0,1},{1,0},{2,3},{3,2},{4,5},{5,4},{6,7},{7,6},{8,9},{9,8},{10,11... | collective-permute-start | bytes 3145736 | tf_op jit(solution)/shard_map/ppermute | solution.py:360
  127.5 13.8 %collective-permute-start.29 = (bf16[2,2,256,256]{3,2,1,0:T(8,128)(2,1)S(1)}, bf16[2,2,256,256]{3,2,1,0:T(8,128)(2,1)S(1)}, u32[]{:S(2)}, u32[]{:S(2)}) collective-permute-start(bf16[2,2,256,256]{3,2,1,0:T(8,128)(2,1)S(1)} %get-tuple-element.208.refs_5_.refs_3_), channel_id=1, source_target_pairs={{0,2},{2,4},{4,6},{3,1},{5,3},{7,5},{8,10},{10,12},{12,14},{11,9},... | collective-permute-start | bytes 1572872 | tf_op jit(solution)/shard_map/ppermute | solution.py:344
  133.3 13.7 %collective-permute-start.30 = (bf16[2,2,256,256]{3,2,1,0:T(8,128)(2,1)S(1)}, bf16[2,2,256,256]{3,2,1,0:T(8,128)(2,1)S(1)}, u32[]{:S(2)}, u32[]{:S(2)}) collective-permute-start(bf16[2,2,256,256]{3,2,1,0:T(8,128)(2,1)S(1)} %get-tuple-element.207.refs_6_.refs_1_), channel_id=1, source_target_pairs={{0,2},{2,4},{4,6},{3,1},{5,3},{7,5},{8,10},{10,12},{12,14},{11,9},... | collective-permute-start | bytes 1572872 | tf_op jit(solution)/shard_map/ppermute | solution.py:344
  137.8 26.1 %collective-permute-start.42 = (bf16[4,2,256,256]{3,2,1,0:T(8,128)(2,1)S(1)}, bf16[4,2,256,256]{3,2,1,0:T(8,128)(2,1)S(1)}, u32[]{:S(2)}, u32[]{:S(2)}) collective-permute-start(bf16[4,2,256,256]{3,2,1,0:T(8,128)(2,1)S(1)} %get-tuple-element.237), channel_id=1, source_target_pairs={{0,16},{8,24},{16,0},{24,8},{1,17},{9,25},{17,1},{25,9},{2,18},{10... | collective-permute-start | bytes 3145736 | tf_op jit(solution)/shard_map/ppermute | solution.py:364
  141.3 24.3 %collective-permute-start.35 = (bf16[4,2,256,256]{3,2,1,0:T(8,128)(2,1)S(1)}, bf16[4,2,256,256]{3,2,1,0:T(8,128)(2,1)S(1)}, u32[]{:S(2)}, u32[]{:S(2)}) collective-permute-start(bf16[4,2,256,256]{3,2,1,0:T(8,128)(2,1)S(1)} %collective-permute-done.34.near_ref), channel_id=1, source_target_pairs={{0,1},{1,0},{2,3},{3,2},{4,5},{5,4},{6,7},{7,6},{8,9},{9,8},{10,11... | collective-permute-start | bytes 3145736 | tf_op jit(solution)/shard_map/ppermute | solution.py:367
  150.3 27.2 %collective-permute-start.39 = (bf16[4,2,256,256]{3,2,1,0:T(8,128)(2,1)S(1)}, bf16[4,2,256,256]{3,2,1,0:T(8,128)(2,1)S(1)}, u32[]{:S(2)}, u32[]{:S(2)}) collective-permute-start(bf16[4,2,256,256]{3,2,1,0:T(8,128)(2,1)S(1)} %get-tuple-element.231), channel_id=1, source_target_pairs={{0,1},{1,0},{2,3},{3,2},{4,5},{5,4},{6,7},{7,6},{8,9},{9,8},{10,11... | collective-permute-start | bytes 3145736 | tf_op jit(solution)/shard_map/ppermute | solution.py:360
  153.7 14.3 %collective-permute-start.36 = (bf16[2,2,256,256]{3,2,1,0:T(8,128)(2,1)S(1)}, bf16[2,2,256,256]{3,2,1,0:T(8,128)(2,1)S(1)}, u32[]{:S(2)}, u32[]{:S(2)}) collective-permute-start(bf16[2,2,256,256]{3,2,1,0:T(8,128)(2,1)S(1)} %get-tuple-element.217.refs_5_.refs_3_), channel_id=1, source_target_pairs={{0,2},{2,4},{4,6},{3,1},{5,3},{7,5},{8,10},{10,12},{12,14},{11,9},... | collective-permute-start | bytes 1572872 | tf_op jit(solution)/shard_map/ppermute | solution.py:344
  159.4 15.0 %collective-permute-start.38 = (bf16[2,2,256,256]{3,2,1,0:T(8,128)(2,1)S(1)}, bf16[2,2,256,256]{3,2,1,0:T(8,128)(2,1)S(1)}, u32[]{:S(2)}, u32[]{:S(2)}) collective-permute-start(bf16[2,2,256,256]{3,2,1,0:T(8,128)(2,1)S(1)} %get-tuple-element.219.refs_6_.refs_1_), channel_id=1, source_target_pairs={{0,2},{2,4},{4,6},{3,1},{5,3},{7,5},{8,10},{10,12},{12,14},{11,9},... | collective-permute-start | bytes 1572872 | tf_op jit(solution)/shard_map/ppermute | solution.py:344
  163.8 27.5 %collective-permute-start.51 = (bf16[4,2,256,256]{3,2,1,0:T(8,128)(2,1)S(1)}, bf16[4,2,256,256]{3,2,1,0:T(8,128)(2,1)S(1)}, u32[]{:S(2)}, u32[]{:S(2)}) collective-permute-start(bf16[4,2,256,256]{3,2,1,0:T(8,128)(2,1)S(1)} %get-tuple-element.254), channel_id=1, source_target_pairs={{0,24},{8,0},{16,8},{24,16},{1,25},{9,1},{17,9},{25,17},{2,26},{10... | collective-permute-start | bytes 3145736 | tf_op jit(solution)/shard_map/ppermute | solution.py:364
  165.6 23.7 %collective-permute-start.43 = (bf16[4,2,256,256]{3,2,1,0:T(8,128)(2,1)S(1)}, bf16[4,2,256,256]{3,2,1,0:T(8,128)(2,1)S(1)}, u32[]{:S(2)}, u32[]{:S(2)}) collective-permute-start(bf16[4,2,256,256]{3,2,1,0:T(8,128)(2,1)S(1)} %collective-permute-done.42.near_ref), channel_id=1, source_target_pairs={{0,1},{1,0},{2,3},{3,2},{4,5},{5,4},{6,7},{7,6},{8,9},{9,8},{10,11... | collective-permute-start | bytes 3145736 | tf_op jit(solution)/shard_map/ppermute | solution.py:367
  177.5 24.0 %collective-permute-start.37 = (bf16[4,2,256,256]{3,2,1,0:T(8,128)(2,1)S(1)}, bf16[4,2,256,256]{3,2,1,0:T(8,128)(2,1)S(1)}, u32[]{:S(2)}, u32[]{:S(2)}) collective-permute-start(bf16[4,2,256,256]{3,2,1,0:T(8,128)(2,1)S(1)} %get-tuple-element.228), channel_id=1, source_target_pairs={{0,1},{1,0},{2,3},{3,2},{4,5},{5,4},{6,7},{7,6},{8,9},{9,8},{10,11... | collective-permute-start | bytes 3145736 | tf_op jit(solution)/shard_map/ppermute | solution.py:360
  179.2 14.5 %collective-permute-start.44 = (bf16[2,2,256,256]{3,2,1,0:T(8,128)(2,1)S(1)}, bf16[2,2,256,256]{3,2,1,0:T(8,128)(2,1)S(1)}, u32[]{:S(2)}, u32[]{:S(2)}) collective-permute-start(bf16[2,2,256,256]{3,2,1,0:T(8,128)(2,1)S(1)} %get-tuple-element.234.refs_5_.refs_3_), channel_id=1, source_target_pairs={{0,2},{2,4},{4,6},{3,1},{5,3},{7,5},{8,10},{10,12},{12,14},{11,9},... | collective-permute-start | bytes 1572872 | tf_op jit(solution)/shard_map/ppermute | solution.py:344
  185.0 13.1 %collective-permute-start.45 = (bf16[2,2,256,256]{3,2,1,0:T(8,128)(2,1)S(1)}, bf16[2,2,256,256]{3,2,1,0:T(8,128)(2,1)S(1)}, u32[]{:S(2)}, u32[]{:S(2)}) collective-permute-start(bf16[2,2,256,256]{3,2,1,0:T(8,128)(2,1)S(1)} %get-tuple-element.236.refs_6_.refs_1_), channel_id=1, source_target_pairs={{0,2},{2,4},{4,6},{3,1},{5,3},{7,5},{8,10},{10,12},{12,14},{11,9},... | collective-permute-start | bytes 1572872 | tf_op jit(solution)/shard_map/ppermute | solution.py:344
  189.3 24.0 %collective-permute-start.58 = (bf16[4,2,256,256]{3,2,1,0:T(8,128)(2,1)S(1)}, bf16[4,2,256,256]{3,2,1,0:T(8,128)(2,1)S(1)}, u32[]{:S(2)}, u32[]{:S(2)}) collective-permute-start(bf16[4,2,256,256]{3,2,1,0:T(8,128)(2,1)S(1)} %get-tuple-element.270), channel_id=1, source_target_pairs={{0,8},{8,16},{16,24},{24,0},{1,9},{9,17},{17,25},{25,1},{2,10},{10... | collective-permute-start | bytes 3145736 | tf_op jit(solution)/shard_map/ppermute | solution.py:364
  191.3 27.0 %collective-permute-start.52 = (bf16[4,2,256,256]{3,2,1,0:T(8,128)(2,1)S(1)}, bf16[4,2,256,256]{3,2,1,0:T(8,128)(2,1)S(1)}, u32[]{:S(2)}, u32[]{:S(2)}) collective-permute-start(bf16[4,2,256,256]{3,2,1,0:T(8,128)(2,1)S(1)} %collective-permute-done.51.near_ref), channel_id=1, source_target_pairs={{0,1},{1,0},{2,3},{3,2},{4,5},{5,4},{6,7},{7,6},{8,9},{9,8},{10,11... | collective-permute-start | bytes 3145736 | tf_op jit(solution)/shard_map/ppermute | solution.py:367
  197.6 23.1 %collective-permute-start.50 = (bf16[4,2,256,256]{3,2,1,0:T(8,128)(2,1)S(1)}, bf16[4,2,256,256]{3,2,1,0:T(8,128)(2,1)S(1)}, u32[]{:S(2)}, u32[]{:S(2)}) collective-permute-start(bf16[4,2,256,256]{3,2,1,0:T(8,128)(2,1)S(1)} %get-tuple-element.253), channel_id=1, source_target_pairs={{0,1},{1,0},{2,3},{3,2},{4,5},{5,4},{6,7},{7,6},{8,9},{9,8},{10,11... | collective-permute-start | bytes 3145736 | tf_op jit(solution)/shard_map/ppermute | solution.py:360
  201.6 11.8 %collective-permute-start.49 = (bf16[2,2,256,256]{3,2,1,0:T(8,128)(2,1)S(1)}, bf16[2,2,256,256]{3,2,1,0:T(8,128)(2,1)S(1)}, u32[]{:S(2)}, u32[]{:S(2)}) collective-permute-start(bf16[2,2,256,256]{3,2,1,0:T(8,128)(2,1)S(1)} %get-tuple-element.248.refs_2_.refs_0_), channel_id=1, source_target_pairs={{0,2},{2,4},{4,6},{3,1},{5,3},{7,5},{8,10},{10,12},{12,14},{11,9},... | collective-permute-start | bytes 1572872 | tf_op jit(solution)/shard_map/ppermute | solution.py:344
  208.2 15.8 %collective-permute-start.53 = (bf16[2,2,256,256]{3,2,1,0:T(8,128)(2,1)S(1)}, bf16[2,2,256,256]{3,2,1,0:T(8,128)(2,1)S(1)}, u32[]{:S(2)}, u32[]{:S(2)}) collective-permute-start(bf16[2,2,256,256]{3,2,1,0:T(8,128)(2,1)S(1)} %get-tuple-element.252.refs_5_.refs_3_), channel_id=1, source_target_pairs={{0,2},{2,4},{4,6},{3,1},{5,3},{7,5},{8,10},{10,12},{12,14},{11,9},... | collective-permute-start | bytes 1572872 | tf_op jit(solution)/shard_map/ppermute | solution.py:344
  213.3 31.5 %collective-permute-start.59 = (bf16[4,2,256,256]{3,2,1,0:T(8,128)(2,1)S(1)}, bf16[4,2,256,256]{3,2,1,0:T(8,128)(2,1)S(1)}, u32[]{:S(2)}, u32[]{:S(2)}) collective-permute-start(bf16[4,2,256,256]{3,2,1,0:T(8,128)(2,1)S(1)} %collective-permute-done.58.near_ref), channel_id=1, source_target_pairs={{0,1},{1,0},{2,3},{3,2},{4,5},{5,4},{6,7},{7,6},{8,9},{9,8},{10,11... | collective-permute-start | bytes 3145736 | tf_op jit(solution)/shard_map/ppermute | solution.py:367
  214.0 16.5 %collective-permute-start.54 = (bf16[2,2,256,256]{3,2,1,0:T(8,128)(2,1)S(1)}, bf16[2,2,256,256]{3,2,1,0:T(8,128)(2,1)S(1)}, u32[]{:S(2)}, u32[]{:S(2)}) collective-permute-start(bf16[2,2,256,256]{3,2,1,0:T(8,128)(2,1)S(1)} %get-tuple-element.251.refs_6_.refs_1_), channel_id=1, source_target_pairs={{0,2},{2,4},{4,6},{3,1},{5,3},{7,5},{8,10},{10,12},{12,14},{11,9},... | collective-permute-start | bytes 1572872 | tf_op jit(solution)/shard_map/ppermute | solution.py:344
  221.5 22.7 %collective-permute-start.62 = (bf16[4,2,256,256]{3,2,1,0:T(8,128)(2,1)S(1)}, bf16[4,2,256,256]{3,2,1,0:T(8,128)(2,1)S(1)}, u32[]{:S(2)}, u32[]{:S(2)}) collective-permute-start(bf16[4,2,256,256]{3,2,1,0:T(8,128)(2,1)S(1)} %get-tuple-element.280), channel_id=1, source_target_pairs={{0,24},{8,0},{16,8},{24,16},{1,25},{9,1},{17,9},{25,17},{2,26},{10... | collective-permute-start | bytes 3145736 | tf_op jit(solution)/shard_map/ppermute | solution.py:364
  230.4 16.8 %collective-permute-start.57 = (bf16[4,2,256,256]{3,2,1,0:T(8,128)(2,1)S(1)}, bf16[4,2,256,256]{3,2,1,0:T(8,128)(2,1)S(1)}, u32[]{:S(2)}, u32[]{:S(2)}) collective-permute-start(bf16[4,2,256,256]{3,2,1,0:T(8,128)(2,1)S(1)} %get-tuple-element.269), channel_id=1, source_target_pairs={{0,1},{1,0},{2,3},{3,2},{4,5},{5,4},{6,7},{7,6},{8,9},{9,8},{10,11... | collective-permute-start | bytes 3145736 | tf_op jit(solution)/shard_map/ppermute | solution.py:360
  231.2 13.0 %collective-permute-start.56 = (bf16[2,2,256,256]{3,2,1,0:T(8,128)(2,1)S(1)}, bf16[2,2,256,256]{3,2,1,0:T(8,128)(2,1)S(1)}, u32[]{:S(2)}, u32[]{:S(2)}) collective-permute-start(bf16[2,2,256,256]{3,2,1,0:T(8,128)(2,1)S(1)} %get-tuple-element.264.refs_2_), channel_id=1, source_target_pairs={{0,2},{2,4},{4,6},{3,1},{5,3},{7,5},{8,10},{10,12},{12,14},{11,9},... | collective-permute-start | bytes 1572872 | tf_op jit(solution)/shard_map/ppermute | solution.py:344
  234.6 13.4 %collective-permute-start.60 = (bf16[2,2,256,256]{3,2,1,0:T(8,128)(2,1)S(1)}, bf16[2,2,256,256]{3,2,1,0:T(8,128)(2,1)S(1)}, u32[]{:S(2)}, u32[]{:S(2)}) collective-permute-start(bf16[2,2,256,256]{3,2,1,0:T(8,128)(2,1)S(1)} %get-tuple-element.266.refs_5_), channel_id=1, source_target_pairs={{0,2},{2,4},{4,6},{3,1},{5,3},{7,5},{8,10},{10,12},{12,14},{11,9},... | collective-permute-start | bytes 1572872 | tf_op jit(solution)/shard_map/ppermute | solution.py:344
  252.5 25.1 %collective-permute-start.46 = (bf16[4,2,256,256]{3,2,1,0:T(8,128)(2,1)S(1)}, bf16[4,2,256,256]{3,2,1,0:T(8,128)(2,1)S(1)}, u32[]{:S(2)}, u32[]{:S(2)}) collective-permute-start(bf16[4,2,256,256]{3,2,1,0:T(8,128)(2,1)S(1)} %get-tuple-element.247), channel_id=1, source_target_pairs={{0,16},{8,24},{16,0},{24,8},{1,17},{9,25},{17,1},{25,9},{2,18},{10... | collective-permute-start | bytes 3145736 | tf_op jit(solution)/shard_map/ppermute | solution.py:364
  253.8 23.9 %collective-permute-start.65 = (bf16[4,2,256,256]{3,2,1,0:T(8,128)(2,1)S(1)}, bf16[4,2,256,256]{3,2,1,0:T(8,128)(2,1)S(1)}, u32[]{:S(2)}, u32[]{:S(2)}) collective-permute-start(bf16[4,2,256,256]{3,2,1,0:T(8,128)(2,1)S(1)} %get-tuple-element.287.near_ref), channel_id=1, source_target_pairs={{0,1},{1,0},{2,3},{3,2},{4,5},{5,4},{6,7},{7,6},{8,9},{9,8},{10,11... | collective-permute-start | bytes 3145736 | tf_op jit(solution)/shard_map/ppermute | solution.py:367
  259.3 23.2 %collective-permute-start.64 = (bf16[4,2,256,256]{3,2,1,0:T(8,128)(2,1)S(1)}, bf16[4,2,256,256]{3,2,1,0:T(8,128)(2,1)S(1)}, u32[]{:S(2)}, u32[]{:S(2)}) collective-permute-start(bf16[4,2,256,256]{3,2,1,0:T(8,128)(2,1)S(1)} %get-tuple-element.286.near_ref), channel_id=1, source_target_pairs={{0,1},{1,0},{2,3},{3,2},{4,5},{5,4},{6,7},{7,6},{8,9},{9,8},{10,11... | collective-permute-start | bytes 3145736 | tf_op jit(solution)/shard_map/ppermute | solution.py:367
  (25 other events, 250.4 us)
